TPU v7x, 256 devices: a whole 4x4x8 slice. The times are simulated.
256 devices in a mesh: wide: 16 (over x, y), medium: 2 (over z_lo), narrow: 8 (over z_hi, core).
Axes of the slice: x: 4, y: 4, z: 8 (z_hi: 4, z_lo: 2; z = z_hi * 2 + z_lo), core: 2. Of those that a mesh axis runs over, the one named last changes fastest.
Arguments:
- obj_tile: float32 [2, 4096, 1024], P(None, ('wide', 'narrow'), 'medium'), may hold values from -4 to 4
- probe: float32 [2, 4, 256, 256], replicated, may hold values from -4 to 4
- amplitude: float32 [16, 2, 8, 256, 256], P('wide', 'medium', 'narrow'), may hold values from 0.2 to 2
- row_offsets: int32 [16, 2, 8], P('wide', 'medium', 'narrow'), may hold values from 0 to 256, as said below
- col_offsets: int32 [16, 2, 8], P('wide', 'medium', 'narrow'), may hold values from 0 to 512, as said below
Outputs:
- object_step: float32 [2, 4096, 1024], P(None, ('wide', 'narrow'), 'medium')
- probe_gradient: float32 [2, 4, 256, 256], replicated
Inputs may be any that keep to these rules, and one draw needn't show every extreme that they name: `row_offsets`: in every tile one position has row offset 0 and another one the largest, 256. `col_offsets`: in every tile one position has column offset 0 and another one the largest, 512.
All inputs are finite; a program needn't handle non-finite values.
Results may differ from a plain program's by a relative error of at most 0.0003.
Values sent between devices are 32-bit elements; how exact they have to be, the bound alone decides.
A program may use at most 128 MiB of HBM per device.

v0:
```python
import math

import jax
import jax.numpy as jnp
from jax import lax
from jax.sharding import PartitionSpec as P

HALO = 128


intensity_floor = 0.1
damping = 4.0
highest = lax.Precision.HIGHEST


def padded(array, sides, width):
    for axis, dim in sides:
        devices, length = (lax.axis_size(axis), array.shape[dim])
        up = [(i, (i + 1) % devices) for i in range(devices - 1)]
        down = [(j, i) for i, j in up]
        last = lax.slice_in_dim(array, length - width, length, axis=dim)
        first = lax.slice_in_dim(array, 0, width, axis=dim)
        before = lax.ppermute(last, axis, up)
        after = lax.ppermute(first, axis, down)
        array = jnp.concatenate([before, array, after], axis=dim)
    return array


def from_behind(value, axis, steps):
    count = lax.axis_size(axis)
    first, last = (max(0, -steps), min(count, count - steps))
    return lax.ppermute(value, axis, [(source, source + steps) for source in range(first, last)])


def dft_tables(frame_size):
    steps = jnp.arange(frame_size, dtype=jnp.int32)
    product = steps[:, None] * steps[None, :] % frame_size
    angle = product.astype(jnp.float32) * (2.0 * math.pi / frame_size)
    scale = 1.0 / math.sqrt(frame_size)
    return (jnp.cos(angle) * scale, jnp.sin(angle) * scale)


def right_times(field, table):
    return jnp.einsum("mab,bc->mac", field, table, precision=highest)


def left_times(table, field):
    return jnp.einsum("ab,mbc->mac", table, field, precision=highest)


def transform(real_part, imag_part, cosine, sine_table, sign):
    mid_re = right_times(real_part, cosine) - sign * right_times(imag_part, sine_table)
    mid_im = right_times(imag_part, cosine) + sign * right_times(real_part, sine_table)
    out_re = left_times(cosine, mid_re) - sign * left_times(sine_table, mid_im)
    out_im = left_times(cosine, mid_im) + sign * left_times(sine_table, mid_re)
    return (out_re, out_im)


def extend(field):
    return padded(field, (("wide", 1), ("medium", 2)), HALO)


def cut_patches(field, row_starts, col_starts, frame_size):

    def one_patch(row_start, col_start):
        return lax.dynamic_slice(
            field, (0, row_start, col_start), (field.shape[0], frame_size, frame_size)
        )

    return jax.vmap(one_patch)(row_starts, col_starts)


def fold_rims(accumulated, tile_rows, tile_cols):
    core = accumulated[:, HALO : HALO + tile_rows, :]
    from_above = from_behind(accumulated[:, HALO + tile_rows :, :], "wide", 1)
    from_below = from_behind(accumulated[:, :HALO, :], "wide", -1)
    core = core.at[:, :HALO, :].add(from_above)
    core = core.at[:, tile_rows - HALO :, :].add(from_below)
    centre = core[:, :, HALO : HALO + tile_cols]
    from_left = from_behind(core[:, :, HALO + tile_cols :], "medium", 1)
    from_right = from_behind(core[:, :, :HALO], "medium", -1)
    centre = centre.at[:, :, :HALO].add(from_left)
    centre = centre.at[:, :, tile_cols - HALO :].add(from_right)
    return centre


def per_device(obj_tile, probe, amplitude, row_offsets, col_offsets):
    whole_tile = lax.all_gather(obj_tile, "narrow", axis=1, tiled=True)
    tile_rows = whole_tile.shape[1]
    tile_cols = whole_tile.shape[2]
    frame_size = probe.shape[-1]
    mode_count = probe.shape[1]
    extended = extend(whole_tile)
    row_starts = row_offsets.reshape(-1)
    col_starts = col_offsets.reshape(-1)
    amplitudes = amplitude.reshape((-1, frame_size, frame_size))
    positions = row_starts.shape[0]
    cosine, sine_table = dft_tables(frame_size)
    patches = cut_patches(extended, row_starts, col_starts, frame_size)
    probe_re = probe[0][None]
    probe_im = probe[1][None]
    patch_re = patches[:, 0][:, None]
    patch_im = patches[:, 1][:, None]
    wave_re = (probe_re * patch_re - probe_im * patch_im).reshape((-1, frame_size, frame_size))
    wave_im = (probe_re * patch_im + probe_im * patch_re).reshape((-1, frame_size, frame_size))
    far_re, far_im = transform(wave_re, wave_im, cosine, sine_table, -1.0)
    far_re = far_re.reshape((positions, mode_count, frame_size, frame_size))
    far_im = far_im.reshape((positions, mode_count, frame_size, frame_size))
    inten = jnp.sum(far_re * far_re + far_im * far_im, axis=1)
    factor = (amplitudes / jnp.sqrt(jnp.maximum(inten, intensity_floor)) - 1.0)[:, None]
    chi_re, chi_im = transform(
        (far_re * factor).reshape((-1, frame_size, frame_size)),
        (far_im * factor).reshape((-1, frame_size, frame_size)),
        cosine,
        sine_table,
        1.0,
    )
    chi_re = chi_re.reshape((positions, mode_count, frame_size, frame_size))
    chi_im = chi_im.reshape((positions, mode_count, frame_size, frame_size))
    grad_re = jnp.sum(probe_re * chi_re + probe_im * chi_im, axis=1)
    grad_im = jnp.sum(probe_re * chi_im - probe_im * chi_re, axis=1)
    lighting = jnp.sum(probe[0] * probe[0] + probe[1] * probe[1], axis=0)
    probe_part = jnp.stack(
        [
            jnp.sum(patch_re * chi_re + patch_im * chi_im, axis=0),
            jnp.sum(patch_re * chi_im - patch_im * chi_re, axis=0),
        ]
    )
    accumulated = jnp.zeros((3, tile_rows + 2 * HALO, tile_cols + 2 * HALO), jnp.float32)
    piece = jnp.stack([grad_re[0], grad_im[0], lighting])
    corner = (0, row_starts[0], col_starts[0])
    accumulated = lax.dynamic_update_slice(accumulated, piece, corner)
    summed = lax.psum(accumulated, "narrow")
    folded = fold_rims(summed, tile_rows, tile_cols)
    direction_full = folded[:2] / (folded[2] + damping)
    share_rows = tile_rows // lax.axis_size("narrow")
    first_row = lax.axis_index("narrow") * share_rows
    direction = lax.dynamic_slice_in_dim(direction_full, first_row, share_rows, 1)
    dir_patches = cut_patches(extend(direction_full), row_starts, col_starts, frame_size)
    dir_re = dir_patches[:, 0][:, None]
    dir_im = dir_patches[:, 1][:, None]
    change_re = probe_re * dir_re - probe_im * dir_im
    change_im = probe_re * dir_im + probe_im * dir_re
    numerator = jnp.sum(change_re * chi_re + change_im * chi_im)
    denominator = jnp.sum(change_re * change_re + change_im * change_im)
    probe_total, numerator, denominator = lax.psum(
        (probe_part, numerator, denominator), ("wide", "medium", "narrow")
    )
    return (numerator / denominator * direction, probe_total)


def solution(mesh):
    in_specs = (
        P(None, ("wide", "narrow"), "medium"),
        P(),
        P("wide", "medium", "narrow", None, None),
        P("wide", "medium", "narrow"),
        P("wide", "medium", "narrow"),
    )
    out_specs = (P(None, ("wide", "narrow"), "medium"), P())
    return jax.shard_map(
        per_device, mesh=mesh, in_specs=in_specs, out_specs=out_specs, check_vma=False
    )
```

profile of v0, /device:TPU:1, one launch (start us, length us, event | category | flops | bytes accessed | tf_op | source)
XLA Modules:
  0.0 689.5 jit_solution(14338329301182497407)
XLA Ops:
  7.9 36.1 %all-gather.2.cloned.1.call-done = f32[2,256,512]{2,1,0:T(8,128)} async-done(((f32[2,32,512]{2,1,0:T(8,128)}), f32[2,256,512]{2,1,0:T(8,128)}) %all-gather.2.cloned.1.call-update) | async-done | bytes 1048592 | tf_op jit(solution)/shard_map/all_gather | solution.py:88
  45.4 2.5 collective-permute-start
  49.2 9.7 %collective-permute-done = f32[2,128,512]{2,1,0:T(8,128)S(1)} collective-permute-done((f32[2,128,512]{2,1,0:T(8,128)S(1)}, f32[2,128,512]{2,1,0:T(8,128)S(1)}, u32[]{:S(2)}, u32[]{:S(2)}) %collective-permute-start) | collective-permute-done | bytes 524320 | tf_op jit(solution)/shard_map/ppermute | solution.py:23
  59.1 3.7 collective-permute-done.1
  63.9 3.8 collective-permute-start.2
  70.2 1.6 copy.96
  73.6 3.4 collective-permute-done.2
  77.1 4.6 collective-permute-done.3
  81.7 1.5 fusion.37
  83.5 2.7 fusion.22
  86.2 2.7 fusion.18
  89.0 2.8 fusion.5
  91.8 3.0 fusion.66
  94.7 2.8 fusion.4
  97.5 2.6 fusion.63
  100.1 2.6 fusion.3
  102.8 2.7 add_reduce_fusion.2
  105.5 2.9 fusion.28
  108.4 2.7 fusion.24
  111.1 2.7 convolution_add_fusion.1
  113.8 2.7 fusion.57
  116.5 2.9 convolution_subtract_fusion.1
  119.5 2.6 fusion.60
  122.1 2.6 convolution_add_fusion
  124.7 4.0 fusion.9
  129.7 2.3 copy.74
  132.0 2.5 broadcast_in_dim.6
  134.5 7.5 %dynamic_update_slice.3 = f32[3,512,768]{2,1,0:T(8,128)} dynamic-update-slice(f32[3,512,768]{2,1,0:T(8,128)} %broadcast_in_dim.6, f32[3,256,256]{2,1,0:T(8,128)} %copy.74, s32[]{:T(128)} %constant.141.clone.1, s32[]{:T(128)S(6)} %select_n.57, s32[]{:T(128)S(6)} %select_n.58) | dynamic-update-slice | bytes 1572868 | tf_op jit(solution)/shard_map/dynamic_update_slice | solution.py:132
  142.1 129.0 %all-reduce.4.cloned.1.call-done = f32[3,512,768]{2,1,0:T(8,128)} async-done(((f32[3,512,768]{2,1,0:T(8,128)}), f32[3,512,768]{2,1,0:T(8,128)}) %all-reduce.4.cloned.1.call-update) | async-done | bytes 4718608 | tf_op jit(solution)/shard_map/psum | solution.py:133
  271.1 2.0 fusion.152
  273.2 2.1 collective-permute-start.4
  275.2 1.7 collective-permute-start.5
  276.9 22.6 %collective-permute-done.4 = f32[3,128,768]{2,1,0:T(8,128)S(1)} collective-permute-done((f32[3,128,768]{2,1,0:T(8,128)S(1)}, f32[3,128,768]{2,1,0:T(8,128)S(1)}, u32[]{:S(2)}, u32[]{:S(2)}) %collective-permute-start.4) | collective-permute-done | bytes 1179680 | tf_op jit(solution)/shard_map/ppermute | solution.py:32
  299.7 3.9 collective-permute-done.5
  303.9 5.1 collective-permute-start.6
  310.9 5.1 collective-permute-done.6
  316.1 3.8 collective-permute-done.7
  322.5 4.8 collective-permute-start.8
  327.3 1.5 pad_maximum_fusion
  328.9 5.4 collective-permute-done.9
  335.2 2.1 pad_maximum_fusion.2
  337.3 2.1 collective-permute-start.10
  340.7 251.1 %all-reduce.6.cloned.1.call-done = f32[2,4,256,256]{2,3,1,0:T(8,128)} async-done(((f32[2,4,256,256]{2,3,1,0:T(8,128)}), f32[2,4,256,256]{2,3,1,0:T(8,128)}) %all-reduce.6.cloned.1.call-update) | async-done | bytes 2097168 | tf_op jit(solution)/shard_map/psum | solution.py:146
  591.8 2.9 copy.79
  594.7 1.6 fusion.32
  598.2 1.8 copy.75
  600.0 2.7 add_reduce_fusion
  602.7 77.8 %all-reduce = (f32[]{:T(128)}, f32[]{:T(128)}) all-reduce(f32[]{:T(128)} %get-tuple-element.81, f32[]{:T(128)} %get-tuple-element.80), channel_id=1, replica_groups=mesh['wide'=16,'medium'=2,'narrow'=8] {'wide','medium','narrow'}, use_global_device_ids=true, to_apply=%region_6.7 | all-reduce | flops 2 | bytes 16 | tf_op jit(solution)/shard_map/psum | solution.py:146
  (60 shorter events, 18.6 us)
Async XLA Ops:
  7.2 36.9 %all-gather.2.cloned.1.call-start = ((), (), s32[]{:S(2)}) async-start(), calls=%async_computation | async-start | bytes 1179648 | tf_op jit(solution)/shard_map/all_gather | solution.py:88
  7.9 263.2 %all-reduce.4.cloned.1.call-start = ((), (), s32[]{:S(2)}) async-start(), calls=%async_computation.1 | async-start | bytes 9437184 | tf_op jit(solution)/shard_map/psum | solution.py:133
  44.0 14.9 %copy-start.6 = (f32[2,256,512]{2,1,0:T(8,128)S(1)}, f32[2,256,512]{2,1,0:T(8,128)}, u32[]{:S(2)}) copy-start(f32[2,256,512]{2,1,0:T(8,128)} %all-gather.2.cloned.1.call-done) | copy-start | bytes 3145732
  45.4 13.5 %collective-permute-start = (f32[2,128,512]{2,1,0:T(8,128)S(1)}, f32[2,128,512]{2,1,0:T(8,128)S(1)}, u32[]{:S(2)}, u32[]{:S(2)}) collective-permute-start(f32[2,128,512]{2,1,0:T(8,128)S(1)} %get-tuple-element.100), channel_id=1, source_target_pairs={{0,16},{16,32},{32,48},{48,64},{64,80},{80,96},{96,112},{112,128},... | collective-permute-start | bytes 1572872 | tf_op jit(solution)/shard_map/ppermute | solution.py:23
  47.9 14.8 %collective-permute-start.1 = (f32[2,128,512]{2,1,0:T(8,128)S(1)}, f32[2,128,512]{2,1,0:T(8,128)S(1)}, u32[]{:S(2)}, u32[]{:S(2)}) collective-permute-start(f32[2,128,512]{2,1,0:T(8,128)S(1)} %get-tuple-element.99), channel_id=1, source_target_pairs={{16,0},{32,16},{48,32},{64,48},{80,64},{96,80},{112,96},{128,112},... | collective-permute-start | bytes 1572872 | tf_op jit(solution)/shard_map/ppermute | solution.py:24
  59.1 10.0 %copy-start.7 = (f32[2,4,256,256]{3,2,1,0:T(8,128)S(1)}, f32[2,4,256,256]{3,2,1,0:T(8,128)}, u32[]{:S(2)}) copy-start(f32[2,4,256,256]{3,2,1,0:T(8,128)} %param.14) | copy-start | bytes 6291460
  62.8 7.4 %copy-start.5 = (f32[2,512,512]{2,1,0:T(8,128)}, f32[2,512,512]{2,1,0:T(8,128)S(1)}, u32[]{:S(2)}) copy-start(f32[2,512,512]{2,1,0:T(8,128)S(1)} %constant_dynamic-update-slice_fusion) | copy-start | bytes 6291460
  63.9 13.1 %collective-permute-start.2 = (f32[2,512,128]{2,1,0:T(8,128)}, f32[2,512,128]{2,1,0:T(8,128)}, u32[]{:S(2)}, u32[]{:S(2)}) collective-permute-start(f32[2,512,128]{2,1,0:T(8,128)} %get-tuple-element.94), channel_id=1, source_target_pairs={{0,8},{1,9},{2,10},{3,11},{4,12},{5,13},{6,14},{7,15},{16,24},{17,... | collective-permute-start | bytes 1572872 | tf_op jit(solution)/shard_map/ppermute | solution.py:23
  67.8 13.9 %collective-permute-start.3 = (f32[2,512,128]{2,1,0:T(8,128)}, f32[2,512,128]{2,1,0:T(8,128)}, u32[]{:S(2)}, u32[]{:S(2)}) collective-permute-start(f32[2,512,128]{2,1,0:T(8,128)} %get-tuple-element.93), channel_id=1, source_target_pairs={{8,0},{9,1},{10,2},{11,3},{12,4},{13,5},{14,6},{15,7},{24,16},{25,... | collective-permute-start | bytes 1572872 | tf_op jit(solution)/shard_map/ppermute | solution.py:24
  70.2 3.3 copy-start.8
  83.5 11.2 %copy-start.2 = (f32[256,256]{0,1:T(8,128)}, f32[256,256]{0,1:T(8,128)S(1)}, u32[]{:S(2)}) copy-start(f32[256,256]{0,1:T(8,128)S(1)} %copy.54) | copy-start | bytes 786436
  124.7 185.6 %copy-start = (f32[4,256,256]{2,1,0:T(8,128)}, f32[4,256,256]{2,1,0:T(8,128)S(1)}, u32[]{:S(2)}) copy-start(f32[4,256,256]{2,1,0:T(8,128)S(1)} %convolution_add_fusion) | copy-start | bytes 3145732
  142.1 449.7 %all-reduce.6.cloned.1.call-start = ((), (), s32[]{:S(2)}) async-start(), calls=%async_computation.2 | async-start | bytes 4194304 | tf_op jit(solution)/shard_map/psum | solution.py:146
  271.1 28.4 %copy-start.1 = (f32[3,512,768]{2,1,0:T(8,128)S(1)}, f32[3,512,768]{2,1,0:T(8,128)}, u32[]{:S(2)}) copy-start(f32[3,512,768]{2,1,0:T(8,128)} %all-reduce.4.cloned.1.call-done) | copy-start | bytes 14155780
  273.2 26.4 %collective-permute-start.4 = (f32[3,128,768]{2,1,0:T(8,128)S(1)}, f32[3,128,768]{2,1,0:T(8,128)S(1)}, u32[]{:S(2)}, u32[]{:S(2)}) collective-permute-start(f32[3,128,768]{2,1,0:T(8,128)S(1)} %get-tuple-element.86), channel_id=1, source_target_pairs={{0,16},{16,32},{32,48},{48,64},{64,80},{80,96},{96,112},{112,128},... | collective-permute-start | bytes 3538952 | tf_op jit(solution)/shard_map/ppermute | solution.py:32
  275.2 24.3 %slice-start = ((f32[3,512,768]{2,1,0:T(8,128)}), f32[3,256,768]{2,1,0:T(8,128)S(1)}, s32[]{:S(2)}) async-start(f32[3,512,768]{2,1,0:T(8,128)} %all-reduce.4.cloned.1.call-done), calls=%async_computation.3 | async-start | bytes 4718592 | tf_op jit(solution)/shard_map/slice | solution.py:74
  275.2 28.3 %collective-permute-start.5 = (f32[3,128,768]{2,1,0:T(8,128)S(1)}, f32[3,128,768]{2,1,0:T(8,128)S(1)}, u32[]{:S(2)}, u32[]{:S(2)}) collective-permute-start(f32[3,128,768]{2,1,0:T(8,128)S(1)} %get-tuple-element.85), channel_id=1, source_target_pairs={{16,0},{32,16},{48,32},{64,48},{80,64},{96,80},{112,96},{128,112},... | collective-permute-start | bytes 3538952 | tf_op jit(solution)/shard_map/ppermute | solution.py:32
  299.7 10.7 %copy-start.3 = (f32[256,256]{0,1:T(8,128)S(1)}, f32[256,256]{0,1:T(8,128)}, u32[]{:S(2)}) copy-start(f32[256,256]{0,1:T(8,128)} %copy-done.2) | copy-start | bytes 786436
  299.7 10.7 %copy-start.4 = (f32[4,256,256]{2,1,0:T(8,128)S(1)}, f32[4,256,256]{2,1,0:T(8,128)}, u32[]{:S(2)}) copy-start(f32[4,256,256]{2,1,0:T(8,128)} %get-tuple-element.107) | copy-start | bytes 3145732
  303.9 12.1 %collective-permute-start.6 = (f32[3,256,128]{2,1,0:T(8,128)S(1)}, f32[3,256,128]{2,1,0:T(8,128)S(1)}, u32[]{:S(2)}, u32[]{:S(2)}) collective-permute-start(f32[3,256,128]{2,1,0:T(8,128)S(1)} %get-tuple-element.90), channel_id=1, source_target_pairs={{0,8},{1,9},{2,10},{3,11},{4,12},{5,13},{6,14},{7,15},{16,24},{17,... | collective-permute-start | bytes 1179656 | tf_op jit(solution)/shard_map/ppermute | solution.py:32
  309.0 10.8 %collective-permute-start.7 = (f32[3,256,128]{2,1,0:T(8,128)S(1)}, f32[3,256,128]{2,1,0:T(8,128)S(1)}, u32[]{:S(2)}, u32[]{:S(2)}) collective-permute-start(f32[3,256,128]{2,1,0:T(8,128)S(1)} %get-tuple-element.89), channel_id=1, source_target_pairs={{8,0},{9,1},{10,2},{11,3},{12,4},{13,5},{14,6},{15,7},{24,16},{25,... | collective-permute-start | bytes 1179656 | tf_op jit(solution)/shard_map/ppermute | solution.py:32
  321.3 13.0 %collective-permute-start.9 = (f32[2,128,512]{2,1,0:T(8,128)}, f32[2,128,512]{2,1,0:T(8,128)}, u32[]{:S(2)}, u32[]{:S(2)}) collective-permute-start(f32[2,128,512]{2,1,0:T(8,128)} %get-tuple-element.98), channel_id=1, source_target_pairs={{16,0},{32,16},{48,32},{64,48},{80,64},{96,80},{112,96},{128,112},... | collective-permute-start | bytes 1572872 | tf_op jit(solution)/shard_map/ppermute | solution.py:24
  322.5 12.6 %collective-permute-start.8 = (f32[2,128,512]{2,1,0:T(8,128)}, f32[2,128,512]{2,1,0:T(8,128)}, u32[]{:S(2)}, u32[]{:S(2)}) collective-permute-start(f32[2,128,512]{2,1,0:T(8,128)} %get-tuple-element.97), channel_id=1, source_target_pairs={{0,16},{16,32},{32,48},{48,64},{64,80},{80,96},{96,112},{112,128},... | collective-permute-start | bytes 1572872 | tf_op jit(solution)/shard_map/ppermute | solution.py:23
  337.3 257.4 %collective-permute-start.10 = (f32[2,512,128]{2,1,0:T(8,128)}, f32[2,512,128]{2,1,0:T(8,128)}, u32[]{:S(2)}, u32[]{:S(2)}) collective-permute-start(f32[2,512,128]{2,1,0:T(8,128)} %get-tuple-element.92), channel_id=1, source_target_pairs={{0,8},{1,9},{2,10},{3,11},{4,12},{5,13},{6,14},{7,15},{16,24},{17,... | collective-permute-start | bytes 1572872 | tf_op jit(solution)/shard_map/ppermute | solution.py:23
  339.4 255.3 %collective-permute-start.11 = (f32[2,512,128]{2,1,0:T(8,128)}, f32[2,512,128]{2,1,0:T(8,128)}, u32[]{:S(2)}, u32[]{:S(2)}) collective-permute-start(f32[2,512,128]{2,1,0:T(8,128)} %get-tuple-element.91), channel_id=1, source_target_pairs={{8,0},{9,1},{10,2},{11,3},{12,4},{13,5},{14,6},{15,7},{24,16},{25,... | collective-permute-start | bytes 1572872 | tf_op jit(solution)/shard_map/ppermute | solution.py:24
Sparse Core Ops, SparseCore 0:
  9.8 34.1 all-gather.1
  142.2 128.8 all-reduce.3
  329.0 262.7 all-reduce.5
where the time goes:
time: 700 us; the launch traced here: 690 us
  waiting for transfers between devices  480 us (69%)
  blocking collectives  77.8 us (11%)
  matrix products  45.1 us (6%)
  starting transfers between devices  28.6 us (4%)
  local copies, waits for them, and re-layouts  28.4 us (4%)
  between operations  17.4 us (2%)
  other arithmetic  12.1 us (2%)
    psum x1, waiting for transfers between devices, per_device(): lax.psum((probe_part, numerator, denominator), ('wide', 'medium', 'narrow'))  251 us
    psum x1, waiting for transfers between devices, per_device(): summed = lax.psum(accumulated, 'narrow')  129 us
    psum x1, blocking collectives, per_device(): lax.psum((probe_part, numerator, denominator), ('wide', 'medium', 'narrow'))  77.8 us
    all_gather x1, waiting for transfers between devices, per_device(): whole_tile = lax.all_gather(obj_tile, 'narrow', axis=1, tiled=True)  36.1 us
    ppermute x4, waiting for transfers between devices, from_behind(): lax.ppermute(value, axis, [(source, source + steps) for source in range(f...  35.4 us
    dot_general x8, matrix products, left_times(): return jnp.einsum('ab,mbc->mac', table, field, precision=highest)  22.8 us
    dot_general x8, matrix products, right_times(): return jnp.einsum('mab,bc->mac', field, table, precision=highest)  22.3 us
    ppermute x4, waiting for transfers between devices, padded(): before = lax.ppermute(last, axis, up)  14.1 us
  transfers between devices with their start and end apart: 15, of which 13 were waited for; matrix products, arithmetic and copies ran while one was open for 2% of the time, Pallas kernels for 0%

commit v1 on v0

v1 whole, which is shorter than its diff:
```python
import functools
import math

import jax
import jax.numpy as jnp
import numpy as np
from jax import lax
from jax.experimental import pallas as pl
from jax.experimental.pallas import tpu as pltpu
from jax.sharding import PartitionSpec as P

MESH = pl.DeviceIdType.MESH
f32 = jnp.float32
bf16 = jnp.bfloat16
FRAME = 256
MODES = 4
HALO = 128
STRIP = 32
NX, NY, NZ = 4, 4, 8
ROW_TILES = 16
INTENSITY_FLOOR = 0.1
DAMPING = 4.0


def here():
    w = lax.axis_index("wide")
    m = lax.axis_index("medium")
    n = lax.axis_index("narrow")
    return w // NY, w % NY, (n // 2) * 2 + m, n % 2


def device(x, y, z, c):
    return (x * NY + y, z % 2, (z // 2) * 2 + c)


class Sends:
    def __init__(self, sem):
        self.sem = sem
        self.copies = []

    def start(self, src, dst, recv_sem, target):
        copy = pltpu.make_async_remote_copy(
            src_ref=src,
            dst_ref=dst,
            send_sem=self.sem.at[len(self.copies)],
            recv_sem=recv_sem,
            device_id=target,
            device_id_type=MESH,
        )
        copy.start()
        self.copies.append(copy)

    def arrived(self, dst, recv_sem, source):
        pltpu.make_async_remote_copy(
            src_ref=dst,
            dst_ref=dst,
            send_sem=self.sem.at[0],
            recv_sem=recv_sem,
            device_id=source,
            device_id_type=MESH,
        ).wait_recv()

    def finish(self):
        for copy in self.copies:
            copy.wait_send()


def greet(peers):
    barrier = pltpu.get_barrier_semaphore()
    for peer in peers:
        pl.semaphore_signal(barrier, inc=1, device_id=peer, device_id_type=MESH)
    pl.semaphore_wait(barrier, len(peers))


def dft_tables():
    steps = np.arange(FRAME)
    angle = (steps[:, None] * steps[None, :] % FRAME) * (2.0 * math.pi / FRAME)
    cosine = np.cos(angle) / math.sqrt(FRAME)
    sine = np.sin(angle) / math.sqrt(FRAME)
    found = []
    for table in (
        np.block([[cosine, -sine], [sine, cosine]]),
        np.block([[cosine, sine], [-sine, cosine]]),
    ):
        table = table.astype(np.float32)
        high = table.astype(jnp.bfloat16)
        found += [high, (table - high.astype(np.float32)).astype(jnp.bfloat16)]
    return np.stack(found)


def split(x):
    high = x.astype(bf16)
    return high, (x - high.astype(f32)).astype(bf16)


def dot(a, b):
    return jnp.dot(a, b, preferred_element_type=f32)


def transform(field, tables, right, left):
    high, low = split(field)
    mid = dot(high, tables[right]) + dot(high, tables[right + 1]) + dot(low, tables[right])
    mid = jnp.concatenate([mid[:, :FRAME], mid[:, FRAME:]], axis=0)
    high, low = split(mid)
    return dot(tables[left], high) + dot(tables[left], low) + dot(tables[left + 1], high)


BLOCKS = ((1, 0), (1, 1), (2, 0), (2, 1), (3, 0), (3, 1), (4, 0), (0, 0))
N_SENDS = 200


def one_hot(shape, hit):
    return jnp.where(hit(lax.broadcasted_iota(jnp.int32, shape, 0), lax.broadcasted_iota(jnp.int32, shape, 1)), 1.0, 0.0).astype(bf16)


def pick_columns(x, table):
    high, low = split(x)
    return dot(high, table) + dot(low, table)


def pick_rows(table, x):
    high, low = split(x)
    return dot(table, high) + dot(table, low)


def update_kernel(
    obj, probe_in, amp_in, tables_in, own_row, offsets,
    step_out, probe_out,
    rows_tile, probe, amp, tables, far, factor, light, grad, where,
    sib_out, sib_in, total, halo_in, ring_in, ring_start, weight, direction,
    probe_part, part_in, part, in1, sum1, in2, sum2, in3, all3, all2, tile, tiles_in,
    send_sem, local_sem, gring_sem, gsib_sem, ghalo_sem, gsibhalo_sem, where_sem,
    sib_sem, halo_sem, ring_sem, part_sem, part_send_sem, sem1, sem2, sem3, asem3, asem2, asem1, asem0,
    tile_sem,
):
    x, y, z, c = here()
    m = z % 2
    w = x * NY + y
    n = (z // 2) * 2 + c
    xs = [((x + i) % NX) for i in range(NX)]
    ys = [((y + i) % NY) for i in range(NY)]
    zs = [((z + i) % NZ) for i in range(NZ)]
    x_peer = [device(v, y, z, c) for v in xs]
    y_peer = [device(x, v, z, c) for v in ys]
    z_peer = [device(x, y, v, c) for v in zs]
    sibling = device(x, y, z, 1 - c)
    up, down = z_peer[1], z_peer[7]
    onward = (up, down)
    behind = (down, up)
    wide_up = ((w + 1) % ROW_TILES, m, n)
    wide_down = ((w + ROW_TILES - 1) % ROW_TILES, m, n)
    sends = Sends(send_sem)

    locals_ = [
        pltpu.make_async_copy(a, b, local_sem.at[i])
        for i, (a, b) in enumerate(
            ((probe_in, probe), (amp_in, amp), (tables_in, tables))
        )
    ]
    for copy in locals_:
        copy.start()
    greet([sibling, wide_up, wide_down] + x_peer[1:] + y_peer[1:] + z_peer[1:])

    def strip_of(zb, core):
        return (zb // 2) * 2 + core

    def place(zb, core):
        rows = pl.ds(pl.multiple_of(HALO + STRIP * strip_of(zb, core), STRIP), STRIP)
        return rows, pl.ds(pl.multiple_of(512 * (zb % 2), 128), 512)

    def halo_place(zb, core, distance):
        s = strip_of(zb, core)
        rows = pl.ds(pl.multiple_of(HALO + STRIP * s + 256 * (1 - 2 * (s // 4)), STRIP), STRIP)
        if distance % 2 == 0:
            return rows, pl.ds(pl.multiple_of(512 * m, 128), 512)
        return rows, pl.ds(pl.multiple_of(512 - 128 * m, 128), 128)

    def block_of(distance, way):
        return (z + NZ - distance) % NZ if way == 0 else (z + distance) % NZ

    def pass_on(slot, src=None):
        distance, way = BLOCKS[slot]
        zb = block_of(distance, way)
        rows, cols = place(zb, c)
        whole = rows_tile.at[:, rows, cols]
        sends.start(whole if src is None else src, whole, gsib_sem.at[slot], sibling)
        hrows, hcols = halo_place(zb, c, distance)
        towards = (w + ROW_TILES + 2 * (strip_of(zb, c) // 4) - 1) % ROW_TILES
        sends.start(
            rows_tile.at[:, rows, hcols] if src is None else src,
            rows_tile.at[:, hrows, hcols], ghalo_sem.at[slot], (towards, m, n),
        )

    rows, cols = place(z, c)
    for plane in range(2):
        for way in range(2):
            sends.start(
                obj.at[plane], rows_tile.at[plane, rows, cols], gring_sem.at[way, 0, plane], onward[way]
            )
    pass_on(7, obj)
    own = pltpu.make_async_copy(obj, rows_tile.at[:, rows, cols], local_sem.at[3])
    own.start()
    mine = where.at[1, pl.ds(8 * c + z, 1)]
    for i in range(1, 8):
        sends.start(own_row, mine, where_sem.at[i - 1], z_peer[i])
    keep = pltpu.make_async_copy(own_row, mine, local_sem.at[4])
    keep.start()

    slot = 0
    for distance in (1, 2, 3):
        for plane in range(2):
            for way in range(2):
                rows, cols = place(block_of(distance, way), c)
                ref = rows_tile.at[plane, rows, cols]
                sends.arrived(ref, gring_sem.at[way, distance - 1, plane], behind[way])
                if distance < 3 or plane == way:
                    sends.start(ref, ref, gring_sem.at[way, distance, plane], onward[way])
        for way in range(2):
            pass_on(slot)
            slot += 1
        if distance == 1:
            keep.wait()
            for i in range(1, 8):
                sends.arrived(where.at[1, pl.ds(8 * c + zs[8 - i], 1)], where_sem.at[i - 1], z_peer[8 - i])
            half = where.at[1, pl.ds(pl.multiple_of(8 * c, 8), 8)]
            sends.start(half, half, where_sem.at[7], sibling)
        if distance == 2:
            sends.arrived(where.at[1, pl.ds(pl.multiple_of(8 * (1 - c), 8), 8)], where_sem.at[7], sibling)
            sends.start(where.at[1], where.at[0], where_sem.at[8], wide_up)
            sends.start(where.at[1], where.at[2], where_sem.at[9], wide_down)
    rows, cols = place(block_of(4, 0), c)
    for way in range(2):
        sends.arrived(rows_tile.at[way, rows, cols], gring_sem.at[way, 3, way], behind[way])
    pass_on(6)
    order = (7, 0, 1, 2, 3, 4, 5, 6)
    for slot in order:
        distance, way = BLOCKS[slot]
        hrows, hcols = halo_place(block_of(distance, way), c, distance)
        ref = rows_tile.at[:, hrows, hcols]
        sends.arrived(ref, ghalo_sem.at[slot], wide_up)
        sends.start(ref, ref, gsibhalo_sem.at[slot], sibling)
    for slot in order:
        distance, way = BLOCKS[slot]
        zb = block_of(distance, way)
        rows, cols = place(zb, 1 - c)
        sends.arrived(rows_tile.at[:, rows, cols], gsib_sem.at[slot], sibling)
        hrows, hcols = halo_place(zb, 1 - c, distance)
        sends.arrived(rows_tile.at[:, hrows, hcols], gsibhalo_sem.at[slot], sibling)
    own.wait()
    for copy in locals_:
        copy.wait()

    r0 = offsets[0]
    c0 = offsets[1] - HALO * (1 - m)

    def on_object(row):
        at = row + (256 * w - HALO)
        return (at >= 0) & (at < 256 * ROW_TILES)

    columns = one_hot((640, FRAME), lambda i, j: i == j + c0)
    lines = one_hot((FRAME, 512), lambda i, j: (j == i + r0) & on_object(j))
    window = pl.ds(pl.multiple_of(384 * m, 128), 640)
    patch = far.at[MODES]

    @pl.loop(0, 2)
    def _(plane):
        narrowed = pick_columns(rows_tile[plane, :, window], columns)
        patch[pl.ds(pl.multiple_of(plane * FRAME, FRAME), FRAME)] = pick_rows(lines, narrowed)

    factor[...] = jnp.zeros_like(factor)
    light[...] = jnp.zeros_like(light)
    grad[...] = jnp.zeros_like(grad)

    @pl.loop(0, MODES)
    def _(k):
        a, b = probe[0, k], probe[1, k]
        pr, pi = patch[:FRAME], patch[FRAME:]
        light[...] += a * a + b * b
        wave = jnp.concatenate([a * pr - b * pi, a * pi + b * pr], axis=1)
        result = transform(wave, tables, 0, 2)
        far[k] = result
        factor[...] += result[:FRAME] * result[:FRAME] + result[FRAME:] * result[FRAME:]

    factor[...] = amp[...] / jnp.sqrt(jnp.maximum(factor[...], INTENSITY_FLOOR)) - 1.0

    def part_copy(k):
        rows = pl.ds(pl.multiple_of(256 * k, 256), 256)
        return pltpu.make_async_remote_copy(
            src_ref=probe_part.at[1 - c, rows], dst_ref=part_in.at[rows],
            send_sem=part_send_sem.at[k], recv_sem=part_sem.at[k],
            device_id=sibling, device_id_type=MESH,
        )

    @pl.loop(0, MODES)
    def _(k):
        scale = factor[...]
        field = jnp.concatenate([far[k, :FRAME] * scale, far[k, FRAME:] * scale], axis=1)
        chi = transform(field, tables, 2, 0)
        cre, cim = chi[:FRAME], chi[FRAME:]
        a, b = probe[0, k], probe[1, k]
        pr, pi = patch[:FRAME], patch[FRAME:]
        grad[0] += a * cre + b * cim
        grad[1] += a * cim - b * cre
        rows = pl.ds(pl.multiple_of(256 * k, 256), 256)
        probe_part[0, rows] = pr * cre + pi * cim
        probe_part[1, rows] = pr * cim - pi * cre
        part_copy(k).start()

    columns_back = one_hot((FRAME, 640), lambda i, j: j == i + c0)

    def put(core, dst):
        lines_back = one_hot(
            (FRAME, FRAME), lambda i, j: 64 * (i // STRIP) + STRIP * core + i % STRIP == j + r0
        )
        for plane in range(2):
            found = pick_columns(pick_rows(lines_back, grad[plane]), columns_back)
            for j in range(8):
                dst[j, plane] = found[STRIP * j : STRIP * (j + 1)]

    put(1 - c, sib_out)
    for k in (0, 3, 1, 2):
        both = pl.ds(2 * k, 2)
        sends.start(sib_out.at[both], sib_in.at[both], sib_sem.at[k], sibling)
    put(c, total)

    def take_parts(half):
        for k in (2 * half, 2 * half + 1):
            rows = pl.ds(256 * k, 256)
            part_copy(k).wait_recv()
            part[rows] = part_in[rows] + probe_part[c, rows]
        for i in range(1, 4):
            q = (xs if half == 0 else ys)[i]
            sends.start(
                part.at[pl.ds(pl.multiple_of(512 * half + 128 * q, 128), 128)],
                in1.at[half, i - 1], sem1.at[half, i - 1],
                (x_peer if half == 0 else y_peer)[i],
            )

    take_parts(0)
    for k in (0, 3, 1, 2):
        both = pl.ds(2 * k, 2)
        sends.arrived(sib_in.at[both], sib_sem.at[k], sibling)
        total[both] += sib_in[both]
        if k in (0, 3):
            for i in range(2):
                sends.start(
                    total.at[2 * k + i], halo_in.at[k // 3, i], halo_sem.at[k // 3, i],
                    wide_down if k == 0 else wide_up,
                )
    take_parts(1)

    light_high, light_low = split(light[...])
    sends.arrived(where.at[0], where_sem.at[8], wide_down)
    sends.arrived(where.at[2], where_sem.at[9], wide_up)
    weight[...] = jnp.zeros_like(weight)

    @pl.loop(0, 48)
    def _(i):
        a = w - 1 + i // 16
        b = i % 2
        at = where[i // 16, i % 16]
        rs = STRIP * n + 256 * (w - a) + HALO - at[:, 0:1]
        cs = 512 * (m - b) + HALO - at[:, 1:2]
        real = (a >= 0) & (a < ROW_TILES)
        lines = one_hot((STRIP, FRAME), lambda p, q: (q == p + rs) & real)
        columns = one_hot((FRAME, 512), lambda p, q: p == q + cs)
        rows = jnp.concatenate([dot(lines, light_high), dot(lines, light_low)], axis=0).astype(bf16)
        found = dot(rows, columns)
        weight[...] += found[:STRIP] + found[STRIP:]

    for side in range(2):
        real = (w < ROW_TILES - 1) if side == 0 else (w > 0)
        for k in range(2):
            sends.arrived(halo_in.at[side, k], halo_sem.at[side, k], wide_up if side == 0 else wide_down)
            j = (4 if side == 0 else 2) + k
            total[j] += jnp.where(real, halo_in[side, k], 0.0)

    def near(zb, plane):
        return total.at[2 + zb // 2, plane, :, pl.ds(pl.multiple_of(128 * m, 128), 512)]

    def further(zb, plane):
        return total[2 + zb // 2, plane, :, pl.ds(pl.multiple_of(512 * (1 - m), 128), 128)]

    far_cols = pl.ds(pl.multiple_of(384 * m, 128), 128)
    for way in range(2):
        sends.start(
            near((z + 4) % NZ, way), ring_in.at[way, 3, way], ring_sem.at[way, 3, way], onward[way]
        )
    ring_start[...] = jnp.zeros_like(ring_start)
    for way in range(2):
        zb = (z + 3) % NZ if way == 0 else (z + NZ - 3) % NZ
        ring_start[way, :, far_cols] = further(zb, 1 - way)
        sends.start(
            ring_start.at[way], ring_in.at[way, 2, 1 - way], ring_sem.at[way, 2, 1 - way], onward[way]
        )

    def ring_step(distance):
        for first in range(2):
            for way in range(2):
                plane = way if first == 0 else 1 - way
                if distance == 3 and plane != way:
                    continue
                zb = (z + distance) % NZ if way == 0 else (z + NZ - distance) % NZ
                slot = ring_in.at[way, distance, plane]
                sends.arrived(slot, ring_sem.at[way, distance, plane], behind[way])
                if distance % 2 == 0:
                    slot[...] += near(zb, plane)[...]
                else:
                    slot[:, far_cols] += further(zb, plane)
                sends.start(
                    slot, ring_in.at[way, distance - 1, plane], ring_sem.at[way, distance - 1, plane], onward[way]
                )

    ring_step(3)
    for half in range(2):
        first = (x if half == 0 else y)
        peers = (x_peer if half == 0 else y_peer)
        for i in range(1, 4):
            sends.arrived(in1.at[half, i - 1], sem1.at[half, i - 1], peers[4 - i])
        rows = pl.ds(pl.multiple_of(512 * half + 128 * first, 128), 128)
        sum1[half] = part[rows] + in1[half, 0] + in1[half, 1] + in1[half, 2]
        for i in range(1, 4):
            q = (ys if half == 0 else xs)[i]
            sends.start(
                sum1.at[half, pl.ds(pl.multiple_of(32 * q, 32), 32)],
                in2.at[half, i - 1], sem2.at[half, i - 1],
                (y_peer if half == 0 else x_peer)[i],
            )
    ring_step(2)
    for half in range(2):
        second = (y if half == 0 else x)
        peers = (y_peer if half == 0 else x_peer)
        for i in range(1, 4):
            sends.arrived(in2.at[half, i - 1], sem2.at[half, i - 1], peers[4 - i])
        rows = pl.ds(pl.multiple_of(32 * second, 32), 32)
        sum2[half] = sum1[half, rows] + in2[half, 0] + in2[half, 1] + in2[half, 2]

    def z_tile(v):
        return pl.ds(pl.multiple_of(8 * (v // 2), 8), 8), pl.ds(pl.multiple_of(128 * (v % 2), 128), 128)

    for i in range(1, 8):
        rows, cols = z_tile(zs[i])
        sends.start(sum2.at[:, rows, cols], in3.at[i - 1], sem3.at[i - 1], z_peer[i])
    ring_step(1)
    for i in range(1, 8):
        sends.arrived(in3.at[i - 1], sem3.at[i - 1], z_peer[8 - i])
    rows, cols = z_tile(z)
    whole = sum2[:, rows, cols]
    for i in range(1, 8):
        whole = whole + in3[i - 1]
    all3[:, rows, cols] = whole
    for i in range(1, 8):
        sends.start(all3.at[:, rows, cols], all3.at[:, rows, cols], asem3.at[i - 1], z_peer[i])

    for way in range(2):
        for plane in range(2):
            sends.arrived(ring_in.at[way, 0, plane], ring_sem.at[way, 0, plane], behind[way])
    numerator = jnp.zeros((), f32)
    under = 1.0 / (weight[...] + DAMPING)
    squares = jnp.zeros((STRIP, 512), f32)
    for plane in range(2):
        strip = near(z, plane)[...] + ring_in[0, 0, plane] + ring_in[1, 0, plane]
        step = strip * under
        direction[plane] = step
        numerator += jnp.sum(step * strip)
        squares += step * step
    denominator = jnp.sum(squares * weight[...])
    line = lax.broadcasted_iota(jnp.int32, (8, 128), 0)
    tile[0] = jnp.where(line == 0, numerator, denominator)

    def tile_send(stage, peers, first):
        for i in range(1, len(peers)):
            sends.start(tile.at[stage], tiles_in.at[first + i - 1], tile_sem.at[first + i - 1], peers[i])

    def tile_sum(stage, peers, first):
        found = tile[stage]
        for i in range(1, len(peers)):
            sends.arrived(tiles_in.at[first + i - 1], tile_sem.at[first + i - 1], peers[len(peers) - i])
        for i in range(1, len(peers)):
            found = found + tiles_in[first + i - 1]
        tile[stage + 1] = found

    tile_send(0, z_peer, 0)

    for i in range(1, 8):
        prows, pcols = z_tile(zs[8 - i])
        sends.arrived(all3.at[:, prows, pcols], asem3.at[i - 1], z_peer[8 - i])
    for half in range(2):
        second = (y if half == 0 else x)
        peers = (y_peer if half == 0 else x_peer)
        rows = pl.ds(pl.multiple_of(32 * second, 32), 32)
        all2[half, rows] = all3[half]
        for i in range(1, 4):
            sends.start(all3.at[half], all2.at[half, rows], asem2.at[half, i - 1], peers[i])
    tile_sum(0, z_peer, 0)
    tile_send(1, y_peer, 7)
    for half in range(2):
        theirs = (ys if half == 0 else xs)
        peers = (y_peer if half == 0 else x_peer)
        for i in range(1, 4):
            rows = pl.ds(pl.multiple_of(32 * theirs[4 - i], 32), 32)
            sends.arrived(all2.at[half, rows], asem2.at[half, i - 1], peers[4 - i])
        first = (x if half == 0 else y)
        peers = (x_peer if half == 0 else y_peer)
        rows = pl.ds(pl.multiple_of(512 * half + 128 * first, 128), 128)
        for i in range(1, 4):
            sends.start(all2.at[half], probe_out.at[c, rows], asem1.at[half, i - 1], peers[i])
        sends.start(all2.at[half], probe_out.at[c, rows], asem0.at[half, 0], sibling)
        probe_out[c, rows] = all2[half]
    tile_sum(1, y_peer, 7)
    tile_send(2, x_peer, 10)
    tile_sum(2, x_peer, 10)
    tile_send(3, [None, sibling], 13)
    for half in range(2):
        theirs = (xs if half == 0 else ys)
        peers = (x_peer if half == 0 else y_peer)
        for i in range(1, 4):
            rows = pl.ds(pl.multiple_of(512 * half + 128 * theirs[4 - i], 128), 128)
            ref = probe_out.at[c, rows]
            sends.arrived(ref, asem1.at[half, i - 1], peers[4 - i])
            sends.start(ref, ref, asem0.at[half, i], sibling)
    tile_sum(3, [None, sibling], 13)
    sums = tile[4]
    alpha = sums[0:1, 0:1] / sums[1:2, 0:1]
    step_out[...] = direction[...] * alpha
    for half in range(2):
        theirs = (xs if half == 0 else ys)
        for i in range(4):
            rows = pl.ds(pl.multiple_of(512 * half + 128 * theirs[(4 - i) % 4], 128), 128)
            sends.arrived(probe_out.at[1 - c, rows], asem0.at[half, i], sibling)
    for k in range(MODES):
        part_copy(k).wait_send()
    sends.finish()


VMEM = pl.BlockSpec(memory_space=pltpu.VMEM)
SMEM = pl.BlockSpec(memory_space=pltpu.SMEM)
ANY = pl.BlockSpec(memory_space=pl.ANY)
DMA = pltpu.SemaphoreType.DMA


def update(obj, probe, amp, tables, own_row, offsets):
    v = lambda *shape: pltpu.VMEM(shape, f32)
    return pl.pallas_call(
        update_kernel,
        out_shape=[
            jax.ShapeDtypeStruct((2, STRIP, 512), f32),
            jax.ShapeDtypeStruct((2, 1024, FRAME), f32),
        ],
        in_specs=[ANY, ANY, ANY, ANY, VMEM, SMEM],
        out_specs=[VMEM, VMEM],
        scratch_shapes=[
            v(2, 512, 1024),
            v(2, MODES, FRAME, FRAME),
            v(FRAME, FRAME),
            pltpu.VMEM((4, 512, 512), bf16),
            v(MODES + 1, 512, FRAME),
            v(FRAME, FRAME),
            v(FRAME, FRAME),
            v(2, FRAME, FRAME),
            pltpu.VMEM((3, 16, 1, 128), jnp.int32),
            v(8, 2, STRIP, 640),
            v(8, 2, STRIP, 640),
            v(8, 2, STRIP, 640),
            v(2, 2, 2, STRIP, 640),
            v(2, 4, 2, STRIP, 512),
            v(2, STRIP, 512),
            v(STRIP, 512),
            v(2, STRIP, 512),
            v(2, 1024, FRAME),
            v(1024, FRAME),
            v(1024, FRAME),
            v(2, 3, 128, FRAME),
            v(2, 128, FRAME),
            v(2, 3, 32, FRAME),
            v(2, 32, FRAME),
            v(7, 2, 8, 128),
            v(2, 32, FRAME),
            v(2, 128, FRAME),
            v(5, 8, 128),
            v(14, 8, 128),
            DMA((N_SENDS,)),
            DMA((5,)),
            DMA((2, 4, 2)),
            DMA((8,)),
            DMA((8,)),
            DMA((8,)),
            DMA((10,)),
            DMA((4,)),
            DMA((2, 2)),
            DMA((2, 4, 2)),
            DMA((MODES,)),
            DMA((MODES,)),
            DMA((2, 3)),
            DMA((2, 3)),
            DMA((7,)),
            DMA((7,)),
            DMA((2, 3)),
            DMA((2, 3)),
            DMA((2, 4)),
            DMA((14,)),
        ],
        compiler_params=pltpu.CompilerParams(
            collective_id=0, has_side_effects=True, vmem_limit_bytes=56 * 2**20
        ),
    )(obj, probe, amp, tables, own_row, offsets)


def per_device(obj_tile, probe, amplitude, row_offsets, col_offsets):
    own = jnp.stack([row_offsets.reshape(()), col_offsets.reshape(())])
    own_row = jnp.pad(own, (0, 126)).reshape((1, 1, 128))
    step, gradient = update(
        obj_tile, probe, amplitude.reshape((FRAME, FRAME)), jnp.asarray(dft_tables()), own_row, own
    )
    return step, gradient.reshape((2, MODES, FRAME, FRAME))


def solution(mesh):
    in_specs = (
        P(None, ("wide", "narrow"), "medium"),
        P(),
        P("wide", "medium", "narrow", None, None),
        P("wide", "medium", "narrow"),
        P("wide", "medium", "narrow"),
    )
    out_specs = (P(None, ("wide", "narrow"), "medium"), P())
    return jax.shard_map(
        per_device, mesh=mesh, in_specs=in_specs, out_specs=out_specs, check_vma=False
    )
```

time: 700 us -> 112 us (0.16); the launches traced: 690 us -> 112 us
  waiting for transfers between devices: 480 us -> 0 us
  Pallas kernels: 0 us -> 105 us
  blocking collectives: 77.8 us -> 0 us
  matrix products: 45.1 us -> 0 us
  starting transfers between devices: 28.6 us -> 0 us
  local copies, waits for them, and re-layouts: 28.4 us -> 5.13 us
  between operations: 17.4 us -> 1.93 us
  other arithmetic: 12.1 us -> 0.08 us
    psum x2 -> x0, waiting for transfers between devices: 380 us -> none  [the longest x1 251 us: per_device(): lax.psum((probe_part, numerator, denominator), ('wide', 'medium', 'narrow'))]
    pallas_call x0 -> x1, Pallas kernels: none -> 105 us  [update(): pl.pallas_call(update_kernel, out_shape=[jax.ShapeDtypeStruct((2, STRIP,...]
    psum x1 -> x0, blocking collectives: 77.8 us -> none  [per_device(): lax.psum((probe_part, numerator, denominator), ('wide', 'medium', 'narrow'))]
    ppermute x12 -> x0, waiting for transfers between devices: 63.2 us -> none  [the longest x4 35.4 us: from_behind(): lax.ppermute(value, axis, [(source, source + steps) for source in range(f...]
    dot_general x16 -> x0, matrix products: 45.1 us -> none  [the longest x8 22.8 us: left_times(): return jnp.einsum('ab,mbc->mac', table, field, precision=highest)]
    all_gather x1 -> x0, waiting for transfers between devices: 36.1 us -> none  [per_device(): whole_tile = lax.all_gather(obj_tile, 'narrow', axis=1, tiled=True)]
    ppermute x12 -> x0, starting transfers between devices: 28.5 us -> none  [the longest x4 13.2 us: padded(): before = lax.ppermute(last, axis, up)]
    dynamic_update_slice x1 -> x0, local copies, waits for them, and re-layouts: 7.54 us -> none  [per_device(): accumulated = lax.dynamic_update_slice(accumulated, piece, corner)]
  transfers between devices with their start and end apart: 15 -> 0, of which waited for: 13 -> 0; matrix products, arithmetic and copies ran while one was open for 2% -> 0% of each run, Pallas kernels for 0% -> 0%
where the time goes in v1:
time: 112 us
  Pallas kernels  105 us (94%)
  local copies, waits for them, and re-layouts  5.13 us (5%)
  between operations  1.93 us (2%)
    pallas_call x1, Pallas kernels, update(): pl.pallas_call(update_kernel, out_shape=[jax.ShapeDtypeStruct((2, STRIP,...  105 us
    unnamed x4, local copies, waits for them, and re-layouts  4.62 us

profile of v1, /device:TPU:1, one launch (start us, length us, event | category | flops | bytes accessed | tf_op | source)
XLA Modules:
  0.0 112.0 jit_solution(12227081536280449488)
XLA Ops:
  1.9 0.1 pad_add_fusion.offsets
  2.0 0.0 copy-start
  2.0 0.5 pad_bitcast_fusion.own_row
  2.5 0.0 copy-done
  2.5 104.9 %shard_map.77 = (f32[2,32,512]{2,1,0:T(8,128)}, f32[2,1024,256]{2,1,0:T(8,128)}) custom-call(f32[2,32,512]{2,1,0:T(8,128)} %obj.1, f32[2,4,256,256]{3,2,1,0:T(8,128)} %probe_in.1, f32[256,256]{1,0:T(8,128)} %bitcast.9, bf16[4,512,512]{2,1,0:T(8,128)(2,1)} %constant.4.clone.tables_in, s32[1,1,128]{2,1,0:T(1,128)} %pad_bitcast_fusion.own_row, s32[2]{0:T(128)} %copy-done), custom_call_target="tpu_custom_call" | custom-call | tf_op jit(solution)/shard_map/pallas_call | solution.py:544
  107.4 1.6 %copy.12 = f32[2,32,512]{2,1,0:T(8,128)} copy(f32[2,32,512]{2,1,0:T(8,128)} %get-tuple-element.8) | data formatting | bytes 262144
  109.0 3.0 %copy.13 = f32[2,4,256,256]{3,2,1,0:T(8,128)} copy(f32[2,4,256,256]{3,2,1,0:T(8,128)} %bitcast.8) | data formatting | bytes 4194304
Async XLA Ops:
  2.0 0.5 copy-start

commit v2 on v1

v2 whole, which is shorter than its diff:
```python
import functools
import math

import jax
import jax.numpy as jnp
import numpy as np
from jax import lax
from jax.experimental import pallas as pl
from jax.experimental.pallas import tpu as pltpu
from jax.sharding import PartitionSpec as P

MESH = pl.DeviceIdType.MESH
f32 = jnp.float32
bf16 = jnp.bfloat16
FRAME = 256
MODES = 4
HALO = 128
STRIP = 32
NX, NY, NZ = 4, 4, 8
ROW_TILES = 16
INTENSITY_FLOOR = 0.1
DAMPING = 4.0


def here():
    w = lax.axis_index("wide")
    m = lax.axis_index("medium")
    n = lax.axis_index("narrow")
    return w // NY, w % NY, (n // 2) * 2 + m, n % 2


def device(x, y, z, c):
    return (x * NY + y, z % 2, (z // 2) * 2 + c)


class Sends:
    def __init__(self, sem):
        self.sem = sem
        self.copies = []

    def start(self, src, dst, recv_sem, target):
        copy = pltpu.make_async_remote_copy(
            src_ref=src,
            dst_ref=dst,
            send_sem=self.sem.at[len(self.copies)],
            recv_sem=recv_sem,
            device_id=target,
            device_id_type=MESH,
        )
        copy.start()
        self.copies.append(copy)

    def arrived(self, dst, recv_sem, source):
        pltpu.make_async_remote_copy(
            src_ref=dst,
            dst_ref=dst,
            send_sem=self.sem.at[0],
            recv_sem=recv_sem,
            device_id=source,
            device_id_type=MESH,
        ).wait_recv()

    def finish(self):
        for copy in self.copies:
            copy.wait_send()


def greet(peers):
    barrier = pltpu.get_barrier_semaphore()
    for peer in peers:
        pl.semaphore_signal(barrier, inc=1, device_id=peer, device_id_type=MESH)
    pl.semaphore_wait(barrier, len(peers))


def dft_tables():
    steps = np.arange(FRAME)
    angle = (steps[:, None] * steps[None, :] % FRAME) * (2.0 * math.pi / FRAME)
    cosine = np.cos(angle) / math.sqrt(FRAME)
    sine = np.sin(angle) / math.sqrt(FRAME)
    found = []
    for table in (
        np.block([[cosine, -sine], [sine, cosine]]),
        np.block([[cosine, sine], [-sine, cosine]]),
    ):
        table = table.astype(np.float32)
        high = table.astype(jnp.bfloat16)
        found += [high, (table - high.astype(np.float32)).astype(jnp.bfloat16)]
    return np.stack(found)


def split(x):
    high = x.astype(bf16)
    return high, (x - high.astype(f32)).astype(bf16)


def dot(a, b):
    return jnp.dot(a, b, preferred_element_type=f32)


def transform(field, tables, right, left):
    high, low = split(field)
    mid = dot(high, tables[right]) + dot(high, tables[right + 1]) + dot(low, tables[right])
    mid = jnp.concatenate([mid[:, :FRAME], mid[:, FRAME:]], axis=0)
    high, low = split(mid)
    return dot(tables[left], high) + dot(tables[left], low) + dot(tables[left + 1], high)


BLOCKS = (0, 6, 2, 7, 1, 3, 5, 4)
N_SENDS = 160


def one_hot(shape, hit):
    return jnp.where(hit(lax.broadcasted_iota(jnp.int32, shape, 0), lax.broadcasted_iota(jnp.int32, shape, 1)), 1.0, 0.0).astype(bf16)


def pick_columns(x, table):
    high, low = split(x)
    return dot(high, table) + dot(low, table)


def pick_rows(table, x):
    high, low = split(x)
    return dot(table, high) + dot(table, low)


def update_kernel(
    obj, probe_in, amp_in, tables_in, row_in, col_in,
    step_out, probe_out,
    rows_tile, probe, amp, tables, far, factor, light, grad, where,
    sib_out, sib_in, total, halo_in, in_four, in_two, in_side, weight, direction,
    probe_part, part_in, part, in1, sum1, in2, sum2, in3, all3, all2, tile, tiles_in,
    send_sem, local_sem, gtwo_sem, gfour_sem, gside_sem, gsib_sem, ghalo_sem, gsibhalo_sem, where_sem,
    sib_sem, halo_sem, four_sem, two_sem, side_sem, part_sem, part_send_sem, sem1, send1_sem, sem2, sem3,
    asem3, asem2, asem1, asem0, tile_sem,
):
    x, y, z, c = here()
    m = z % 2
    zh = z // 2
    w = x * NY + y
    n = zh * 2 + c
    xs = [((x + i) % NX) for i in range(NX)]
    ys = [((y + i) % NY) for i in range(NY)]
    zs = [((z + i) % NZ) for i in range(NZ)]
    x_peer = [device(v, y, z, c) for v in xs]
    y_peer = [device(x, v, z, c) for v in ys]
    z_peer = [device(x, y, v, c) for v in zs]
    plane_peer = [((w + i) % ROW_TILES, m, n) for i in range(ROW_TILES)]
    sibling = device(x, y, z, 1 - c)
    wide_up, wide_down = plane_peer[1], plane_peer[15]
    onward = (z_peer[2], z_peer[6])
    behind = (z_peer[6], z_peer[2])
    sends = Sends(send_sem)

    locals_ = [
        pltpu.make_async_copy(a, b, local_sem.at[i])
        for i, (a, b) in enumerate(
            ((probe_in, probe), (amp_in, amp), (tables_in, tables))
        )
    ]
    for copy in locals_:
        copy.start()
    r0 = row_in[0, 0, 0]
    offset_col = col_in[0, 0, 0]
    c0 = offset_col - HALO * (1 - m)
    lane = lax.broadcasted_iota(jnp.int32, (1, 128), 1)
    where[1, 8 * c + z] = jnp.where(lane == 0, r0, offset_col)
    greet([sibling] + plane_peer[1:] + z_peer[1:])

    def strip_of(zb, core):
        return (zb // 2) * 2 + core

    own_cols = pl.ds(pl.multiple_of(128 * m, 128), 512)
    side_cols = pl.ds(pl.multiple_of(512 * (1 - m), 128), 128)

    def columns_of(distance):
        return side_cols if distance % 2 else own_cols

    def place(zb, core):
        return pl.ds(pl.multiple_of(HALO + STRIP * strip_of(zb, core), STRIP), STRIP)

    def halo_place(zb, core):
        s = strip_of(zb, core)
        return pl.ds(pl.multiple_of(HALO + STRIP * s + 256 * (1 - 2 * (s // 4)), STRIP), STRIP)

    def pass_on(slot, src=None):
        distance = BLOCKS[slot]
        zb = zs[distance]
        cols = columns_of(distance)
        ref = rows_tile.at[:, place(zb, c), cols]
        towards = (w + ROW_TILES + 2 * (strip_of(zb, c) // 4) - 1) % ROW_TILES
        sends.start(
            ref if src is None else src,
            rows_tile.at[:, halo_place(zb, c), cols], ghalo_sem.at[slot], (towards, m, n),
        )
        sends.start(ref if src is None else src, ref, gsib_sem.at[slot], sibling)

    rows = place(z, c)
    for plane in range(2):
        for way in range(2):
            p = plane if way == 0 else 1 - plane
            sends.start(
                obj.at[p], rows_tile.at[p, rows, own_cols], gtwo_sem.at[way, p], onward[way]
            )
    pass_on(0, obj)
    out_cols = pl.ds(pl.multiple_of(384 * (1 - m), 128), 128)
    there = pl.ds(pl.multiple_of(512 * m, 128), 128)
    for i, distance in enumerate((1, 7, 3, 5)):
        sends.start(
            obj.at[:, :, out_cols], rows_tile.at[:, rows, there], gside_sem.at[i], z_peer[distance]
        )
    own = pltpu.make_async_copy(obj, rows_tile.at[:, rows, own_cols], local_sem.at[3])
    own.start()
    mine = where.at[1, pl.ds(8 * c + z, 1)]
    for i in range(1, 8):
        sends.start(mine, mine, where_sem.at[i - 1], z_peer[i])


    locals_[0].wait()
    light[...] = jnp.zeros_like(light)

    @pl.loop(0, MODES)
    def _(k):
        light[...] += probe[0, k] * probe[0, k] + probe[1, k] * probe[1, k]

    weight[...] = jnp.zeros_like(weight)

    def lamp(t):
        light_high, light_low = split(light[...])
        a = w - 1 + t
        real = (a >= 0) & (a < ROW_TILES)

        def add(i, b, first, width):
            at = where[t, 8 * (i // 4) + 2 * (i % 4) + b]
            rs = STRIP * n + 256 * (1 - t) + HALO - at[:, 0:1]
            cs = 512 * (m - b) + first + HALO - at[:, 1:2]
            lines = one_hot((STRIP, FRAME), lambda p, q: (q == p + rs) & real)
            columns = one_hot((FRAME, width), lambda p, q: p == q + cs)
            rows = jnp.concatenate([dot(lines, light_high), dot(lines, light_low)], axis=0).astype(bf16)
            found = dot(rows, columns)
            return found[:STRIP] + found[STRIP:]

        @pl.loop(0, 8)
        def _(i):
            weight[...] += add(i, m, 0, 512)
            weight[:, out_cols] += add(i, 1 - m, 384 * (1 - m), 128)

    for i in range(1, 8):
        sends.arrived(where.at[1, pl.ds(8 * c + zs[8 - i], 1)], where_sem.at[i - 1], z_peer[8 - i])
    half = where.at[1, pl.ds(pl.multiple_of(8 * c, 8), 8)]
    sends.start(half, half, where_sem.at[7], sibling)
    sends.arrived(where.at[1, pl.ds(pl.multiple_of(8 * (1 - c), 8), 8)], where_sem.at[7], sibling)
    sends.start(where.at[1], where.at[0], where_sem.at[8], wide_up)
    sends.start(where.at[1], where.at[2], where_sem.at[9], wide_down)
    lamp(1)

    for way in range(2):
        zb = zs[6 if way == 0 else 2]
        ref = rows_tile.at[way, place(zb, c), own_cols]
        sends.arrived(ref, gtwo_sem.at[way, way], behind[way])
        sends.start(ref, ref, gfour_sem.at[way], onward[way])
    for way in range(2):
        zb = zs[6 if way == 0 else 2]
        sends.arrived(rows_tile.at[1 - way, place(zb, c), own_cols], gtwo_sem.at[way, 1 - way], behind[way])
        pass_on(1 + way)
    for i, distance in enumerate((7, 1, 5, 3)):
        sends.arrived(rows_tile.at[:, place(zs[distance], c), side_cols], gside_sem.at[i], z_peer[distance])
        pass_on(BLOCKS.index(distance))

    def halo_arrived(slot):
        distance = BLOCKS[slot]
        ref = rows_tile.at[:, halo_place(zs[distance], c), columns_of(distance)]
        sends.arrived(ref, ghalo_sem.at[slot], wide_up)
        sends.start(ref, ref, gsibhalo_sem.at[slot], sibling)

    halo_arrived(0)
    sends.arrived(where.at[0], where_sem.at[8], wide_down)
    lamp(0)
    for way in range(2):
        sends.arrived(rows_tile.at[way, place(zs[4], c), own_cols], gfour_sem.at[way], behind[way])
    pass_on(7)
    sends.arrived(where.at[2], where_sem.at[9], wide_up)
    lamp(2)
    for slot in range(1, 7):
        halo_arrived(slot)
    halo_arrived(7)
    for slot in range(8):
        distance = BLOCKS[slot]
        cols = columns_of(distance)
        sends.arrived(rows_tile.at[:, place(zs[distance], 1 - c), cols], gsib_sem.at[slot], sibling)
        sends.arrived(rows_tile.at[:, halo_place(zs[distance], 1 - c), cols], gsibhalo_sem.at[slot], sibling)
    own.wait()
    for copy in locals_[1:]:
        copy.wait()

    def on_object(row):
        at = row + (256 * w - HALO)
        return (at >= 0) & (at < 256 * ROW_TILES)

    columns = one_hot((640, FRAME), lambda i, j: i == j + c0)
    lines = one_hot((FRAME, 512), lambda i, j: (j == i + r0) & on_object(j))
    patch = far.at[MODES]

    @pl.loop(0, 2)
    def _(plane):
        narrowed = pick_columns(rows_tile[plane], columns)
        patch[pl.ds(pl.multiple_of(plane * FRAME, FRAME), FRAME)] = pick_rows(lines, narrowed)

    factor[...] = jnp.zeros_like(factor)
    grad[...] = jnp.zeros_like(grad)

    @pl.loop(0, MODES)
    def _(k):
        a, b = probe[0, k], probe[1, k]
        pr, pi = patch[:FRAME], patch[FRAME:]
        wave = jnp.concatenate([a * pr - b * pi, a * pi + b * pr], axis=1)
        result = transform(wave, tables, 0, 2)
        far[k] = result
        factor[...] += result[:FRAME] * result[:FRAME] + result[FRAME:] * result[FRAME:]

    factor[...] = amp[...] / jnp.sqrt(jnp.maximum(factor[...], INTENSITY_FLOOR)) - 1.0

    def part_copy(k):
        return pltpu.make_async_remote_copy(
            src_ref=probe_part.at[1 - c, k], dst_ref=part_in.at[k],
            send_sem=part_send_sem.at[k], recv_sem=part_sem.at[k],
            device_id=sibling, device_id_type=MESH,
        )

    def first_copy(k, i):
        h = k // 2
        tx, ty = (x + i * h) % NX, (y + i * (1 - h)) % NY
        q = h * tx + (1 - h) * ty
        return pltpu.make_async_remote_copy(
            src_ref=part.at[k, pl.ds(pl.multiple_of(64 * q, 64), 64)], dst_ref=in1.at[k, i - 1],
            send_sem=send1_sem.at[k, i - 1], recv_sem=sem1.at[k, i - 1],
            device_id=(tx * NY + ty, m, n), device_id_type=MESH,
        )

    def take_part(k):
        part_copy(k).wait_recv()
        part[k] = part_in[k] + probe_part[c, k]
        for i in range(1, 4):
            first_copy(k, i).start()

    @pl.loop(0, MODES)
    def _(k):
        scale = factor[...]
        field = jnp.concatenate([far[k, :FRAME] * scale, far[k, FRAME:] * scale], axis=1)
        chi = transform(field, tables, 2, 0)
        cre, cim = chi[:FRAME], chi[FRAME:]
        a, b = probe[0, k], probe[1, k]
        pr, pi = patch[:FRAME], patch[FRAME:]
        grad[0] += a * cre + b * cim
        grad[1] += a * cim - b * cre
        probe_part[0, k] = pr * cre + pi * cim
        probe_part[1, k] = pr * cim - pi * cre
        part_copy(k).start()

        @pl.when(k > 0)
        def _():
            take_part(k - 1)

    columns_back = one_hot((FRAME, 640), lambda i, j: j == i + c0)

    def put(core, dst):
        lines_back = one_hot(
            (FRAME, FRAME), lambda i, j: 64 * (i // STRIP) + STRIP * core + i % STRIP == j + r0
        )
        for plane in range(2):
            found = pick_columns(pick_rows(lines_back, grad[plane]), columns_back)
            for j in range(8):
                dst[j, plane] = found[STRIP * j : STRIP * (j + 1)]

    put(1 - c, sib_out)
    for k in (0, 3, 1, 2):
        both = pl.ds(2 * k, 2)
        sends.start(sib_out.at[both], sib_in.at[both], sib_sem.at[k], sibling)
    put(c, total)
    take_part(3)
    early = zh % 2
    for k in (0, 3, 1, 2):
        both = pl.ds(2 * k, 2)
        sends.arrived(sib_in.at[both], sib_sem.at[k], sibling)
        total[both] += sib_in[both]
        if k == 3:
            for i in (early, 1 - early):
                sends.start(total.at[i], halo_in.at[0, i], halo_sem.at[0, i], wide_down)
                sends.start(total.at[6 + i], halo_in.at[1, i], halo_sem.at[1, i], wide_up)

    def take_halo(i):
        for side in range(2):
            real = (w < ROW_TILES - 1) if side == 0 else (w > 0)
            sends.arrived(halo_in.at[side, i], halo_sem.at[side, i], wide_up if side == 0 else wide_down)
            total[(4 if side == 0 else 2) + i] += jnp.where(real, halo_in[side, i], 0.0)

    def block(zb):
        return total.at[2 + zb // 2, :, :, own_cols]

    def second_stage(half):
        first = (y if half == 0 else x)
        peers = (y_peer if half == 0 else x_peer)
        rows = pl.ds(pl.multiple_of(64 * first, 64), 64)
        for k in (2 * half, 2 * half + 1):
            for i in range(1, 4):
                first_copy(k, i).wait_recv()
            sum1[k] = part[k, rows] + in1[k, 0] + in1[k, 1] + in1[k, 2]
        both = pl.ds(2 * half, 2)
        for i in range(1, 4):
            q = (xs if half == 0 else ys)[i]
            sends.start(
                sum1.at[both, pl.ds(pl.multiple_of(16 * q, 16), 16)],
                in2.at[half, i - 1], sem2.at[half, i - 1],
                (x_peer if half == 0 else y_peer)[i],
            )

    second_stage(0)
    second_stage(1)
    take_halo(early)
    for way in range(2):
        sends.start(block(zs[4]).at[way], in_four.at[way], four_sem.at[way], onward[way])

    for half in range(2):
        second = (x if half == 0 else y)
        peers = (x_peer if half == 0 else y_peer)
        for i in range(1, 4):
            sends.arrived(in2.at[half, i - 1], sem2.at[half, i - 1], peers[4 - i])
        rows = pl.ds(pl.multiple_of(16 * second, 16), 16)
        both = pl.ds(2 * half, 2)
        sum2[both] = sum1[both, rows] + in2[half, 0] + in2[half, 1] + in2[half, 2]

    def z_tile(v):
        return (
            pl.ds(2 * (v // 4), 2),
            pl.ds(pl.multiple_of(8 * ((v // 2) % 2), 8), 8),
            pl.ds(pl.multiple_of(128 * (v % 2), 128), 128),
        )

    for i in range(1, 8):
        sends.start(sum2.at[z_tile(zs[i])], in3.at[i - 1], sem3.at[i - 1], z_peer[i])
    take_halo(1 - early)
    for way in range(2):
        sends.start(
            block(zs[2 if way == 0 else 6]).at[1 - way], in_two.at[way, 1 - way], two_sem.at[way, 1 - way], onward[way]
        )
    for i, distance in enumerate((1, 7, 3, 5)):
        sends.start(
            total.at[2 + zs[distance] // 2, :, :, side_cols], in_side.at[i], side_sem.at[i], z_peer[distance]
        )
    for i in range(1, 8):
        sends.arrived(in3.at[i - 1], sem3.at[i - 1], z_peer[8 - i])
    whole = sum2[z_tile(z)]
    for i in range(1, 8):
        whole = whole + in3[i - 1]
    all3[z_tile(z)] = whole
    for i in range(1, 8):
        ref = all3.at[z_tile(z)]
        sends.start(ref, ref, asem3.at[i - 1], z_peer[i])
    for way in range(2):
        sends.arrived(in_four.at[way], four_sem.at[way], behind[way])
        in_four[way] += block(zs[2 if way == 0 else 6])[way]
        sends.start(in_four.at[way], in_two.at[way, way], two_sem.at[way, way], onward[way])

    for i in range(1, 8):
        sends.arrived(all3.at[z_tile(zs[8 - i])], asem3.at[i - 1], z_peer[8 - i])
    for half in range(2):
        second = (x if half == 0 else y)
        peers = (x_peer if half == 0 else y_peer)
        rows = pl.ds(pl.multiple_of(16 * second, 16), 16)
        both = pl.ds(2 * half, 2)
        all2[both, rows] = all3[both]
        for i in range(1, 4):
            sends.start(all3.at[both], all2.at[both, rows], asem2.at[half, i - 1], peers[i])

    near = pl.ds(pl.multiple_of(384 - 256 * m, 128), 128)
    for i, distance in enumerate((7, 1, 5, 3)):
        sends.arrived(in_side.at[i], side_sem.at[i], z_peer[distance])
    total[2 + zh, :, :, near] += in_side[0] + in_side[1] + in_side[2] + in_side[3]
    for way in range(2):
        for plane in range(2):
            sends.arrived(in_two.at[way, plane], two_sem.at[way, plane], behind[way])
    numerator = jnp.zeros((), f32)
    under = 1.0 / (weight[...] + DAMPING)
    squares = jnp.zeros((STRIP, 512), f32)
    for plane in range(2):
        strip = total[2 + zh, plane, :, own_cols] + in_two[0, plane] + in_two[1, plane]
        step = strip * under
        direction[plane] = step
        numerator += jnp.sum(step * strip)
        squares += step * step
    denominator = jnp.sum(squares * weight[...])
    line = lax.broadcasted_iota(jnp.int32, (8, 128), 0)
    tile[0] = jnp.where(line == 0, numerator, denominator)

    def tile_send(stage, peers, first):
        for i in range(1, len(peers)):
            sends.start(tile.at[stage], tiles_in.at[first + i - 1], tile_sem.at[first + i - 1], peers[i])

    def tile_sum(stage, peers, first):
        for i in range(1, len(peers)):
            sends.arrived(tiles_in.at[first + i - 1], tile_sem.at[first + i - 1], peers[len(peers) - i])
        found = tile[stage]
        for i in range(1, len(peers)):
            found = found + tiles_in[first + i - 1]
        tile[stage + 1] = found

    tile_send(0, [None, sibling], 0)
    tile_sum(0, [None, sibling], 0)
    tile_send(1, plane_peer, 1)
    for half in range(2):
        theirs = (xs if half == 0 else ys)
        peers = (x_peer if half == 0 else y_peer)
        both = pl.ds(2 * half, 2)
        for i in range(1, 4):
            rows = pl.ds(pl.multiple_of(16 * theirs[4 - i], 16), 16)
            sends.arrived(all2.at[both, rows], asem2.at[half, i - 1], peers[4 - i])
        first = (y if half == 0 else x)
        peers = (y_peer if half == 0 else x_peer)
        rows = pl.ds(pl.multiple_of(64 * first, 64), 64)
        for i in range(1, 4):
            sends.start(all2.at[both], probe_out.at[c, both, rows], asem1.at[half, i - 1], peers[i])
        sends.start(all2.at[both], probe_out.at[c, both, rows], asem0.at[half, 0], sibling)
        probe_out[c, both, rows] = all2[both]
    tile_sum(1, plane_peer, 1)
    tile_send(2, z_peer, 16)
    tile_sum(2, z_peer, 16)
    sums = tile[3]
    alpha = sums[0:1, 0:1] / sums[1:2, 0:1]
    step_out[...] = direction[...] * alpha
    for half in range(2):
        theirs = (ys if half == 0 else xs)
        peers = (y_peer if half == 0 else x_peer)
        both = pl.ds(2 * half, 2)
        for i in range(1, 4):
            rows = pl.ds(pl.multiple_of(64 * theirs[4 - i], 64), 64)
            ref = probe_out.at[c, both, rows]
            sends.arrived(ref, asem1.at[half, i - 1], peers[4 - i])
            sends.start(ref, ref, asem0.at[half, i], sibling)
    for half in range(2):
        theirs = (ys if half == 0 else xs)
        both = pl.ds(2 * half, 2)
        for i in range(4):
            rows = pl.ds(pl.multiple_of(64 * theirs[(4 - i) % 4], 64), 64)
            sends.arrived(probe_out.at[1 - c, both, rows], asem0.at[half, i], sibling)
    for k in range(MODES):
        part_copy(k).wait_send()
        for i in range(1, 4):
            first_copy(k, i).wait_send()
    sends.finish()


VMEM = pl.BlockSpec(memory_space=pltpu.VMEM)
SMEM = pl.BlockSpec(memory_space=pltpu.SMEM)
ANY = pl.BlockSpec(memory_space=pl.ANY)
DMA = pltpu.SemaphoreType.DMA


def update(obj, probe, amp, tables, row, col):
    v = lambda *shape: pltpu.VMEM(shape, f32)
    return pl.pallas_call(
        update_kernel,
        out_shape=[
            pltpu.VMEM((2, STRIP, 512), f32),
            pltpu.VMEM((2, MODES, FRAME, FRAME), f32),
        ],
        in_specs=[ANY, ANY, ANY, ANY, SMEM, SMEM],
        out_specs=[VMEM, VMEM],
        scratch_shapes=[
            v(2, 512, 640),
            v(2, MODES, FRAME, FRAME),
            v(FRAME, FRAME),
            pltpu.VMEM((4, 512, 512), bf16),
            v(MODES + 1, 512, FRAME),
            v(FRAME, FRAME),
            v(FRAME, FRAME),
            v(2, FRAME, FRAME),
            pltpu.VMEM((3, 16, 1, 128), jnp.int32),
            v(8, 2, STRIP, 640),
            v(8, 2, STRIP, 640),
            v(8, 2, STRIP, 640),
            v(2, 2, 2, STRIP, 640),
            v(2, STRIP, 512),
            v(2, 2, STRIP, 512),
            v(4, 2, STRIP, 128),
            v(STRIP, 512),
            v(2, STRIP, 512),
            v(2, MODES, FRAME, FRAME),
            v(MODES, FRAME, FRAME),
            v(MODES, FRAME, FRAME),
            v(MODES, 3, 64, FRAME),
            v(MODES, 64, FRAME),
            v(2, 3, 2, 16, FRAME),
            v(MODES, 16, FRAME),
            v(7, 2, 8, 128),
            v(MODES, 16, FRAME),
            v(MODES, 64, FRAME),
            v(4, 8, 128),
            v(23, 8, 128),
            DMA((N_SENDS,)),
            DMA((4,)),
            DMA((2, 2)),
            DMA((2,)),
            DMA((4,)),
            DMA((8,)),
            DMA((8,)),
            DMA((8,)),
            DMA((10,)),
            DMA((4,)),
            DMA((2, 2)),
            DMA((2,)),
            DMA((2, 2)),
            DMA((4,)),
            DMA((MODES,)),
            DMA((MODES,)),
            DMA((MODES, 3)),
            DMA((MODES, 3)),
            DMA((2, 3)),
            DMA((7,)),
            DMA((7,)),
            DMA((2, 3)),
            DMA((2, 3)),
            DMA((2, 4)),
            DMA((23,)),
        ],
        compiler_params=pltpu.CompilerParams(
            collective_id=0, has_side_effects=True, vmem_limit_bytes=56 * 2**20
        ),
    )(obj, probe, amp, tables, row, col)


def per_device(obj_tile, probe, amplitude, row_offsets, col_offsets):
    step, gradient = update(
        obj_tile, probe, amplitude.reshape((FRAME, FRAME)), jnp.asarray(dft_tables()), row_offsets, col_offsets
    )
    return step, gradient


def solution(mesh):
    in_specs = (
        P(None, ("wide", "narrow"), "medium"),
        P(),
        P("wide", "medium", "narrow", None, None),
        P("wide", "medium", "narrow"),
        P("wide", "medium", "narrow"),
    )
    out_specs = (P(None, ("wide", "narrow"), "medium"), P())
    return jax.shard_map(
        per_device, mesh=mesh, in_specs=in_specs, out_specs=out_specs, check_vma=False
    )
```

time: 112 us -> 103 us (0.920)
  Pallas kernels: 105 us -> 98.8 us
  local copies, waits for them, and re-layouts: 5.13 us -> 1.98 us
    pallas_call x1, Pallas kernels: 105 us -> 98.8 us  [update(): pl.pallas_call(update_kernel, out_shape=[pltpu.VMEM((2, STRIP, 512), f32)...]
    unnamed x4 -> x2, local copies, waits for them, and re-layouts: 4.62 us -> 1.98 us
where the time goes in v2:
time: 103 us
  Pallas kernels  98.8 us (96%)
  local copies, waits for them, and re-layouts  1.98 us (2%)
  between operations  1.93 us (2%)
    pallas_call x1, Pallas kernels, update(): pl.pallas_call(update_kernel, out_shape=[pltpu.VMEM((2, STRIP, 512), f32)...  98.8 us

profile of v2, /device:TPU:1, one launch (start us, length us, event | category | flops | bytes accessed | tf_op | source)
XLA Modules:
  0.0 102.7 jit_solution(4408345983794793401)
XLA Ops:
  1.9 98.8 %shard_map.77 = (f32[2,32,512]{2,1,0:T(8,128)S(1)}, f32[2,4,256,256]{3,2,1,0:T(8,128)S(1)}) custom-call(f32[2,32,512]{2,1,0:T(8,128)} %obj.1, f32[2,4,256,256]{3,2,1,0:T(8,128)} %probe_in.1, f32[256,256]{1,0:T(8,128)} %bitcast.1, bf16[4,512,512]{2,1,0:T(8,128)(2,1)} %constant.2.clone.tables_in, s32[1,1,1]{2,1,0:T(1,128)S(6)} %copy.12.row_in, ...), custom_call_target="tpu_custom_call" | custom-call | tf_op jit(solution)/shard_map/pallas_call | solution.py:559
  100.7 0.7 copy.10
  101.4 1.3 %copy.11 = f32[2,4,256,256]{3,2,1,0:T(8,128)} copy(f32[2,4,256,256]{3,2,1,0:T(8,128)S(1)} %get-tuple-element.3) | data formatting | bytes 4194304

commit v3 on v2

--- a/solution.py
+++ b/solution.py
@@ -69,7 +69,10 @@
     barrier = pltpu.get_barrier_semaphore()
     for peer in peers:
         pl.semaphore_signal(barrier, inc=1, device_id=peer, device_id_type=MESH)
-    pl.semaphore_wait(barrier, len(peers))
+
+
+def met(peers):
+    pl.semaphore_wait(pltpu.get_barrier_semaphore(), len(peers))
 
 
 def dft_tables():
@@ -78,10 +81,7 @@
     cosine = np.cos(angle) / math.sqrt(FRAME)
     sine = np.sin(angle) / math.sqrt(FRAME)
     found = []
-    for table in (
-        np.block([[cosine, -sine], [sine, cosine]]),
-        np.block([[cosine, sine], [-sine, cosine]]),
-    ):
+    for table in (cosine, cosine + sine, cosine - sine):
         table = table.astype(np.float32)
         high = table.astype(jnp.bfloat16)
         found += [high, (table - high.astype(np.float32)).astype(jnp.bfloat16)]
@@ -97,12 +97,24 @@
     return jnp.dot(a, b, preferred_element_type=f32)
 
 
-def transform(field, tables, right, left):
-    high, low = split(field)
-    mid = dot(high, tables[right]) + dot(high, tables[right + 1]) + dot(low, tables[right])
-    mid = jnp.concatenate([mid[:, :FRAME], mid[:, FRAME:]], axis=0)
-    high, low = split(mid)
-    return dot(tables[left], high) + dot(tables[left], low) + dot(tables[left + 1], high)
+def side(re, im, product, sign):
+    k1 = product(re + im, 0)
+    k2 = product(re, 2 if sign > 0 else 4)
+    k3 = product(im, 4 if sign > 0 else 2)
+    return k1 - k3, k1 - k2
+
+
+def transform(re, im, tables, sign):
+    def right(x, t):
+        high, low = split(x)
+        return dot(high, tables[t]) + dot(high, tables[t + 1]) + dot(low, tables[t])
+
+    def left(x, t):
+        high, low = split(x)
+        return dot(tables[t], high) + dot(tables[t], low) + dot(tables[t + 1], high)
+
+    re, im = side(re, im, right, sign)
+    return side(re, im, left, sign)
 
 
 BLOCKS = (0, 6, 2, 7, 1, 3, 5, 4)
@@ -127,7 +139,7 @@
     obj, probe_in, amp_in, tables_in, row_in, col_in,
     step_out, probe_out,
     rows_tile, probe, amp, tables, far, factor, light, grad, where,
-    sib_out, sib_in, total, halo_in, in_four, in_two, in_side, weight, direction,
+    sib_out, sib_in, total, halo_in, in_four, in_two, in_side, weight, direction, lit,
     probe_part, part_in, part, in1, sum1, in2, sum2, in3, all3, all2, tile, tiles_in,
     send_sem, local_sem, gtwo_sem, gfour_sem, gside_sem, gsib_sem, ghalo_sem, gsibhalo_sem, where_sem,
     sib_sem, halo_sem, four_sem, two_sem, side_sem, part_sem, part_send_sem, sem1, send1_sem, sem2, sem3,
@@ -149,6 +161,7 @@
     wide_up, wide_down = plane_peer[1], plane_peer[15]
     onward = (z_peer[2], z_peer[6])
     behind = (z_peer[6], z_peer[2])
+    near_peer = (z_peer[1], z_peer[7])
     sends = Sends(send_sem)
 
     locals_ = [
@@ -164,7 +177,16 @@
     c0 = offset_col - HALO * (1 - m)
     lane = lax.broadcasted_iota(jnp.int32, (1, 128), 1)
     where[1, 8 * c + z] = jnp.where(lane == 0, r0, offset_col)
-    greet([sibling] + plane_peer[1:] + z_peer[1:])
+    everyone = [sibling] + plane_peer[1:] + z_peer[1:]
+    greet(everyone)
+    locals_[0].wait()
+    light[...] = jnp.zeros_like(light)
+
+    @pl.loop(0, MODES)
+    def _(k):
+        light[...] += probe[0, k] * probe[0, k] + probe[1, k] * probe[1, k]
+
+    met(everyone)
 
     def strip_of(zb, core):
         return (zb // 2) * 2 + core
@@ -193,6 +215,10 @@
             rows_tile.at[:, halo_place(zb, c), cols], ghalo_sem.at[slot], (towards, m, n),
         )
         sends.start(ref if src is None else src, ref, gsib_sem.at[slot], sibling)
+
+    mine = where.at[1, pl.ds(8 * c + z, 1)]
+    for i in range(1, 8):
+        sends.start(mine, mine, where_sem.at[i - 1], z_peer[i])
 
     rows = place(z, c)
     for plane in range(2):
@@ -204,67 +230,36 @@
     pass_on(0, obj)
     out_cols = pl.ds(pl.multiple_of(384 * (1 - m), 128), 128)
     there = pl.ds(pl.multiple_of(512 * m, 128), 128)
-    for i, distance in enumerate((1, 7, 3, 5)):
-        sends.start(
-            obj.at[:, :, out_cols], rows_tile.at[:, rows, there], gside_sem.at[i], z_peer[distance]
-        )
+    give_cols = pl.ds(pl.multiple_of(384 - 256 * m, 128), 128)
+    for way in range(2):
+        sends.start(obj.at[:, :, out_cols], rows_tile.at[:, rows, there], gside_sem.at[way, 0], near_peer[way])
     own = pltpu.make_async_copy(obj, rows_tile.at[:, rows, own_cols], local_sem.at[3])
     own.start()
-    mine = where.at[1, pl.ds(8 * c + z, 1)]
-    for i in range(1, 8):
-        sends.start(mine, mine, where_sem.at[i - 1], z_peer[i])
-
-
-    locals_[0].wait()
-    light[...] = jnp.zeros_like(light)
-
-    @pl.loop(0, MODES)
-    def _(k):
-        light[...] += probe[0, k] * probe[0, k] + probe[1, k] * probe[1, k]
-
-    weight[...] = jnp.zeros_like(weight)
-
-    def lamp(t):
-        light_high, light_low = split(light[...])
-        a = w - 1 + t
-        real = (a >= 0) & (a < ROW_TILES)
-
-        def add(i, b, first, width):
-            at = where[t, 8 * (i // 4) + 2 * (i % 4) + b]
-            rs = STRIP * n + 256 * (1 - t) + HALO - at[:, 0:1]
-            cs = 512 * (m - b) + first + HALO - at[:, 1:2]
-            lines = one_hot((STRIP, FRAME), lambda p, q: (q == p + rs) & real)
-            columns = one_hot((FRAME, width), lambda p, q: p == q + cs)
-            rows = jnp.concatenate([dot(lines, light_high), dot(lines, light_low)], axis=0).astype(bf16)
-            found = dot(rows, columns)
-            return found[:STRIP] + found[STRIP:]
-
-        @pl.loop(0, 8)
-        def _(i):
-            weight[...] += add(i, m, 0, 512)
-            weight[:, out_cols] += add(i, 1 - m, 384 * (1 - m), 128)
+    for way in range(2):
+        zb = zs[6 if way == 0 else 2]
+        ref = rows_tile.at[way, place(zb, c), own_cols]
+        sends.arrived(ref, gtwo_sem.at[way, way], behind[way])
+        sends.start(ref, ref, gfour_sem.at[way], onward[way])
+    for way in range(2):
+        zb = zs[6 if way == 0 else 2]
+        sends.arrived(rows_tile.at[1 - way, place(zb, c), own_cols], gtwo_sem.at[way, 1 - way], behind[way])
+        sends.start(
+            rows_tile.at[:, place(zb, c), give_cols], rows_tile.at[:, place(zb, c), there],
+            gside_sem.at[way, 1], near_peer[way],
+        )
+        pass_on(1 + way)
+    for step in range(2):
+        for way in range(2):
+            distance = ((7, 5), (1, 3))[way][step]
+            sends.arrived(
+                rows_tile.at[:, place(zs[distance], c), side_cols], gside_sem.at[way, step], near_peer[1 - way]
+            )
+            pass_on(BLOCKS.index(distance))
 
     for i in range(1, 8):
         sends.arrived(where.at[1, pl.ds(8 * c + zs[8 - i], 1)], where_sem.at[i - 1], z_peer[8 - i])
     half = where.at[1, pl.ds(pl.multiple_of(8 * c, 8), 8)]
     sends.start(half, half, where_sem.at[7], sibling)
-    sends.arrived(where.at[1, pl.ds(pl.multiple_of(8 * (1 - c), 8), 8)], where_sem.at[7], sibling)
-    sends.start(where.at[1], where.at[0], where_sem.at[8], wide_up)
-    sends.start(where.at[1], where.at[2], where_sem.at[9], wide_down)
-    lamp(1)
-
-    for way in range(2):
-        zb = zs[6 if way == 0 else 2]
-        ref = rows_tile.at[way, place(zb, c), own_cols]
-        sends.arrived(ref, gtwo_sem.at[way, way], behind[way])
-        sends.start(ref, ref, gfour_sem.at[way], onward[way])
-    for way in range(2):
-        zb = zs[6 if way == 0 else 2]
-        sends.arrived(rows_tile.at[1 - way, place(zb, c), own_cols], gtwo_sem.at[way, 1 - way], behind[way])
-        pass_on(1 + way)
-    for i, distance in enumerate((7, 1, 5, 3)):
-        sends.arrived(rows_tile.at[:, place(zs[distance], c), side_cols], gside_sem.at[i], z_peer[distance])
-        pass_on(BLOCKS.index(distance))
 
     def halo_arrived(slot):
         distance = BLOCKS[slot]
@@ -273,15 +268,14 @@
         sends.start(ref, ref, gsibhalo_sem.at[slot], sibling)
 
     halo_arrived(0)
-    sends.arrived(where.at[0], where_sem.at[8], wide_down)
-    lamp(0)
     for way in range(2):
         sends.arrived(rows_tile.at[way, place(zs[4], c), own_cols], gfour_sem.at[way], behind[way])
     pass_on(7)
-    sends.arrived(where.at[2], where_sem.at[9], wide_up)
-    lamp(2)
     for slot in range(1, 7):
         halo_arrived(slot)
+    sends.arrived(where.at[1, pl.ds(pl.multiple_of(8 * (1 - c), 8), 8)], where_sem.at[7], sibling)
+    sends.start(where.at[1], where.at[0], where_sem.at[8], wide_up)
+    sends.start(where.at[1], where.at[2], where_sem.at[9], wide_down)
     halo_arrived(7)
     for slot in range(8):
         distance = BLOCKS[slot]
@@ -305,17 +299,14 @@
         narrowed = pick_columns(rows_tile[plane], columns)
         patch[pl.ds(pl.multiple_of(plane * FRAME, FRAME), FRAME)] = pick_rows(lines, narrowed)
 
-    factor[...] = jnp.zeros_like(factor)
-    grad[...] = jnp.zeros_like(grad)
-
-    @pl.loop(0, MODES)
-    def _(k):
+    pr, pi = patch[:FRAME], patch[FRAME:]
+    for k in range(MODES):
         a, b = probe[0, k], probe[1, k]
-        pr, pi = patch[:FRAME], patch[FRAME:]
-        wave = jnp.concatenate([a * pr - b * pi, a * pi + b * pr], axis=1)
-        result = transform(wave, tables, 0, 2)
-        far[k] = result
-        factor[...] += result[:FRAME] * result[:FRAME] + result[FRAME:] * result[FRAME:]
+        fre, fim = transform(a * pr - b * pi, a * pi + b * pr, tables, 1)
+        far[k, :FRAME] = fre
+        far[k, FRAME:] = fim
+        squares = fre * fre + fim * fim
+        factor[...] = squares if k == 0 else factor[...] + squares
 
     factor[...] = amp[...] / jnp.sqrt(jnp.maximum(factor[...], INTENSITY_FLOOR)) - 1.0
 
@@ -342,22 +333,18 @@
         for i in range(1, 4):
             first_copy(k, i).start()
 
-    @pl.loop(0, MODES)
-    def _(k):
+    for k in range(MODES):
         scale = factor[...]
-        field = jnp.concatenate([far[k, :FRAME] * scale, far[k, FRAME:] * scale], axis=1)
-        chi = transform(field, tables, 2, 0)
-        cre, cim = chi[:FRAME], chi[FRAME:]
+        cre, cim = transform(far[k, :FRAME] * scale, far[k, FRAME:] * scale, tables, -1)
         a, b = probe[0, k], probe[1, k]
         pr, pi = patch[:FRAME], patch[FRAME:]
-        grad[0] += a * cre + b * cim
-        grad[1] += a * cim - b * cre
         probe_part[0, k] = pr * cre + pi * cim
         probe_part[1, k] = pr * cim - pi * cre
         part_copy(k).start()
-
-        @pl.when(k > 0)
-        def _():
+        gre, gim = a * cre + b * cim, a * cim - b * cre
+        grad[0] = gre if k == 0 else grad[0] + gre
+        grad[1] = gim if k == 0 else grad[1] + gim
+        if k > 0:
             take_part(k - 1)
 
     columns_back = one_hot((FRAME, 640), lambda i, j: j == i + c0)
@@ -387,6 +374,34 @@
                 sends.start(total.at[i], halo_in.at[0, i], halo_sem.at[0, i], wide_down)
                 sends.start(total.at[6 + i], halo_in.at[1, i], halo_sem.at[1, i], wide_up)
 
+    weight[...] = jnp.zeros_like(weight)
+
+    def lamp(t):
+        light_high, light_low = split(light[...])
+        a = w - 1 + t
+        real = (a >= 0) & (a < ROW_TILES)
+        shape = (16, STRIP, FRAME)
+        rs = STRIP * n + 256 * (1 - t) + HALO - where[t][:, :, 0:1]
+        hit = (lax.broadcasted_iota(jnp.int32, shape, 2) == lax.broadcasted_iota(jnp.int32, shape, 1) + rs) & real
+        lines = jnp.where(hit, 1.0, 0.0).reshape((16 * STRIP, FRAME)).astype(bf16)
+        lit[:, 0] = dot(lines, light_high).astype(bf16).reshape(shape)
+        lit[:, 1] = dot(lines, light_low).astype(bf16).reshape(shape)
+
+        def add(i, b, first, width):
+            at = 8 * (i // 4) + 2 * (i % 4) + b
+            cs = 512 * (m - b) + first + HALO - where[t, at][:, 1:2]
+            columns = one_hot((FRAME, width), lambda p, q: p == q + cs)
+            found = dot(lit[at].reshape((2 * STRIP, FRAME)), columns)
+            return found[:STRIP] + found[STRIP:]
+
+        @pl.loop(0, 8)
+        def _(i):
+            weight[...] += add(i, m, 0, 512)
+            weight[:, out_cols] += add(i, 1 - m, 384 * (1 - m), 128)
+
+    lamp(1)
+    sends.arrived(where.at[0], where_sem.at[8], wide_down)
+
     def take_halo(i):
         for side in range(2):
             real = (w < ROW_TILES - 1) if side == 0 else (w > 0)
@@ -446,6 +461,8 @@
         sends.start(
             total.at[2 + zs[distance] // 2, :, :, side_cols], in_side.at[i], side_sem.at[i], z_peer[distance]
         )
+    lamp(0)
+    sends.arrived(where.at[2], where_sem.at[9], wide_up)
     for i in range(1, 8):
         sends.arrived(in3.at[i - 1], sem3.at[i - 1], z_peer[8 - i])
     whole = sum2[z_tile(z)]
@@ -470,6 +487,22 @@
         all2[both, rows] = all3[both]
         for i in range(1, 4):
             sends.start(all3.at[both], all2.at[both, rows], asem2.at[half, i - 1], peers[i])
+
+    lamp(2)
+    for half in range(2):
+        theirs = (xs if half == 0 else ys)
+        peers = (x_peer if half == 0 else y_peer)
+        both = pl.ds(2 * half, 2)
+        for i in range(1, 4):
+            rows = pl.ds(pl.multiple_of(16 * theirs[4 - i], 16), 16)
+            sends.arrived(all2.at[both, rows], asem2.at[half, i - 1], peers[4 - i])
+        first = (y if half == 0 else x)
+        peers = (y_peer if half == 0 else x_peer)
+        rows = pl.ds(pl.multiple_of(64 * first, 64), 64)
+        for i in range(1, 4):
+            sends.start(all2.at[both], probe_out.at[c, both, rows], asem1.at[half, i - 1], peers[i])
+        sends.start(all2.at[both], probe_out.at[c, both, rows], asem0.at[half, 0], sibling)
+        probe_out[c, both, rows] = all2[both]
 
     near = pl.ds(pl.multiple_of(384 - 256 * m, 128), 128)
     for i, distance in enumerate((7, 1, 5, 3)):
@@ -506,20 +539,6 @@
     tile_send(0, [None, sibling], 0)
     tile_sum(0, [None, sibling], 0)
     tile_send(1, plane_peer, 1)
-    for half in range(2):
-        theirs = (xs if half == 0 else ys)
-        peers = (x_peer if half == 0 else y_peer)
-        both = pl.ds(2 * half, 2)
-        for i in range(1, 4):
-            rows = pl.ds(pl.multiple_of(16 * theirs[4 - i], 16), 16)
-            sends.arrived(all2.at[both, rows], asem2.at[half, i - 1], peers[4 - i])
-        first = (y if half == 0 else x)
-        peers = (y_peer if half == 0 else x_peer)
-        rows = pl.ds(pl.multiple_of(64 * first, 64), 64)
-        for i in range(1, 4):
-            sends.start(all2.at[both], probe_out.at[c, both, rows], asem1.at[half, i - 1], peers[i])
-        sends.start(all2.at[both], probe_out.at[c, both, rows], asem0.at[half, 0], sibling)
-        probe_out[c, both, rows] = all2[both]
     tile_sum(1, plane_peer, 1)
     tile_send(2, z_peer, 16)
     tile_sum(2, z_peer, 16)
@@ -568,7 +587,7 @@
             v(2, 512, 640),
             v(2, MODES, FRAME, FRAME),
             v(FRAME, FRAME),
-            pltpu.VMEM((4, 512, 512), bf16),
+            pltpu.VMEM((6, FRAME, FRAME), bf16),
             v(MODES + 1, 512, FRAME),
             v(FRAME, FRAME),
             v(FRAME, FRAME),
@@ -583,6 +602,7 @@
             v(4, 2, STRIP, 128),
             v(STRIP, 512),
             v(2, STRIP, 512),
+            pltpu.VMEM((16, 2, STRIP, FRAME), bf16),
             v(2, MODES, FRAME, FRAME),
             v(MODES, FRAME, FRAME),
             v(MODES, FRAME, FRAME),
@@ -599,7 +619,7 @@
             DMA((4,)),
             DMA((2, 2)),
             DMA((2,)),
-            DMA((4,)),
+            DMA((2, 2)),
             DMA((8,)),
             DMA((8,)),
             DMA((8,)),

time: 103 us -> 98.5 us (0.956)
  Pallas kernels: 98.8 us -> 94.5 us
    pallas_call x1, Pallas kernels: 98.8 us -> 94.5 us  [update(): pl.pallas_call(update_kernel, out_shape=[pltpu.VMEM((2, STRIP, 512), f32)...]
where the time goes in v3:
time: 98.5 us; the launch traced here: 98.4 us
  Pallas kernels  94.5 us (96%)
  local copies, waits for them, and re-layouts  1.98 us (2%)
  between operations  1.93 us (2%)
    pallas_call x1, Pallas kernels, update(): pl.pallas_call(update_kernel, out_shape=[pltpu.VMEM((2, STRIP, 512), f32)...  94.5 us
    unnamed x2, local copies, waits for them, and re-layouts  1.98 us

profile of v3, /device:TPU:1, one launch (start us, length us, event | category | flops | bytes accessed | tf_op | source)
XLA Modules:
  0.0 98.4 jit_solution(2011876503683001376)
XLA Ops:
  1.9 94.5 %shard_map.77 = (f32[2,32,512]{2,1,0:T(8,128)S(1)}, f32[2,4,256,256]{3,2,1,0:T(8,128)S(1)}) custom-call(f32[2,32,512]{2,1,0:T(8,128)} %obj.1, f32[2,4,256,256]{3,2,1,0:T(8,128)} %probe_in.1, f32[256,256]{1,0:T(8,128)} %bitcast.1, bf16[6,256,256]{2,1,0:T(8,128)(2,1)} %constant.2.clone.tables_in, s32[1,1,1]{2,1,0:T(1,128)S(6)} %copy.12.row_in, ...), custom_call_target="tpu_custom_call" | custom-call | tf_op jit(solution)/shard_map/pallas_call | solution.py:578
  96.4 0.7 copy.10
  97.1 1.3 %copy.11 = f32[2,4,256,256]{3,2,1,0:T(8,128)} copy(f32[2,4,256,256]{3,2,1,0:T(8,128)S(1)} %get-tuple-element.3) | data formatting | bytes 4194304

commit v4 on v3

--- a/solution.py
+++ b/solution.py
@@ -118,30 +118,20 @@
 
 
 BLOCKS = (0, 6, 2, 7, 1, 3, 5, 4)
-N_SENDS = 160
+N_SENDS = 192
 
 
 def one_hot(shape, hit):
     return jnp.where(hit(lax.broadcasted_iota(jnp.int32, shape, 0), lax.broadcasted_iota(jnp.int32, shape, 1)), 1.0, 0.0).astype(bf16)
-
-
-def pick_columns(x, table):
-    high, low = split(x)
-    return dot(high, table) + dot(low, table)
-
-
-def pick_rows(table, x):
-    high, low = split(x)
-    return dot(table, high) + dot(table, low)
 
 
 def update_kernel(
     obj, probe_in, amp_in, tables_in, row_in, col_in,
     step_out, probe_out,
-    rows_tile, probe, amp, tables, far, factor, light, grad, where,
+    rows_tile, probe, amp, tables, narrowed, far, factor, light, grad, where,
     sib_out, sib_in, total, halo_in, in_four, in_two, in_side, weight, direction, lit,
-    probe_part, part_in, part, in1, sum1, in2, sum2, in3, all3, all2, tile, tiles_in,
-    send_sem, local_sem, gtwo_sem, gfour_sem, gside_sem, gsib_sem, ghalo_sem, gsibhalo_sem, where_sem,
+    probe_part, part_in, part, in1, sum1, in2, sum2, in3, all3, tile, tiles_in,
+    send_sem, local_sem, gtwo_sem, gfour_sem, gcorner_sem, gside_sem, gsib_sem, ghalo_sem, gsibhalo_sem, where_sem,
     sib_sem, halo_sem, four_sem, two_sem, side_sem, part_sem, part_send_sem, sem1, send1_sem, sem2, sem3,
     asem3, asem2, asem1, asem0, tile_sem,
 ):
@@ -177,7 +167,11 @@
     c0 = offset_col - HALO * (1 - m)
     lane = lax.broadcasted_iota(jnp.int32, (1, 128), 1)
     where[1, 8 * c + z] = jnp.where(lane == 0, r0, offset_col)
-    everyone = [sibling] + plane_peer[1:] + z_peer[1:]
+    def beside(row_tile, way):
+        return (row_tile % ROW_TILES, m, (zs[2 if way == 0 else 6] // 2) * 2 + c)
+
+    corners = [beside(w + 1, 0), beside(w + 1, 1), beside(w + ROW_TILES - 1, 0), beside(w + ROW_TILES - 1, 1)]
+    everyone = [sibling] + plane_peer[1:] + z_peer[1:] + corners
     greet(everyone)
     locals_[0].wait()
     light[...] = jnp.zeros_like(light)
@@ -203,17 +197,20 @@
     def halo_place(zb, core):
         s = strip_of(zb, core)
         return pl.ds(pl.multiple_of(HALO + STRIP * s + 256 * (1 - 2 * (s // 4)), STRIP), STRIP)
+
+    def towards(zb):
+        return (w + ROW_TILES + 2 * (strip_of(zb, c) // 4) - 1) % ROW_TILES
 
     def pass_on(slot, src=None):
         distance = BLOCKS[slot]
         zb = zs[distance]
         cols = columns_of(distance)
         ref = rows_tile.at[:, place(zb, c), cols]
-        towards = (w + ROW_TILES + 2 * (strip_of(zb, c) // 4) - 1) % ROW_TILES
-        sends.start(
-            ref if src is None else src,
-            rows_tile.at[:, halo_place(zb, c), cols], ghalo_sem.at[slot], (towards, m, n),
-        )
+        if distance != 4:
+            sends.start(
+                ref if src is None else src,
+                rows_tile.at[:, halo_place(zb, c), cols], ghalo_sem.at[slot], (towards(zb), m, n),
+            )
         sends.start(ref if src is None else src, ref, gsib_sem.at[slot], sibling)
 
     mine = where.at[1, pl.ds(8 * c + z, 1)]
@@ -240,6 +237,12 @@
         ref = rows_tile.at[way, place(zb, c), own_cols]
         sends.arrived(ref, gtwo_sem.at[way, way], behind[way])
         sends.start(ref, ref, gfour_sem.at[way], onward[way])
+    for way in range(2):
+        zb = zs[6 if way == 0 else 2]
+        sends.start(
+            rows_tile.at[way, place(zb, c), own_cols], rows_tile.at[way, halo_place(zb, c), own_cols],
+            gcorner_sem.at[way], beside(towards(zb), way),
+        )
     for way in range(2):
         zb = zs[6 if way == 0 else 2]
         sends.arrived(rows_tile.at[1 - way, place(zb, c), own_cols], gtwo_sem.at[way, 1 - way], behind[way])
@@ -276,15 +279,10 @@
     sends.arrived(where.at[1, pl.ds(pl.multiple_of(8 * (1 - c), 8), 8)], where_sem.at[7], sibling)
     sends.start(where.at[1], where.at[0], where_sem.at[8], wide_up)
     sends.start(where.at[1], where.at[2], where_sem.at[9], wide_down)
-    halo_arrived(7)
     for slot in range(8):
         distance = BLOCKS[slot]
-        cols = columns_of(distance)
-        sends.arrived(rows_tile.at[:, place(zs[distance], 1 - c), cols], gsib_sem.at[slot], sibling)
-        sends.arrived(rows_tile.at[:, halo_place(zs[distance], 1 - c), cols], gsibhalo_sem.at[slot], sibling)
+        sends.arrived(rows_tile.at[:, place(zs[distance], 1 - c), columns_of(distance)], gsib_sem.at[slot], sibling)
     own.wait()
-    for copy in locals_[1:]:
-        copy.wait()
 
     def on_object(row):
         at = row + (256 * w - HALO)
@@ -294,10 +292,28 @@
     lines = one_hot((FRAME, 512), lambda i, j: (j == i + r0) & on_object(j))
     patch = far.at[MODES]
 
-    @pl.loop(0, 2)
-    def _(plane):
-        narrowed = pick_columns(rows_tile[plane], columns)
-        patch[pl.ds(pl.multiple_of(plane * FRAME, FRAME), FRAME)] = pick_rows(lines, narrowed)
+    def narrow(rows):
+        for plane in range(2):
+            for part, value in enumerate(split(rows_tile[plane, rows])):
+                narrowed[plane, part, rows] = dot(value, columns).astype(bf16)
+
+    narrow(slice(HALO, HALO + 256))
+    corner_rows = halo_place(zs[4], c)
+    for way in range(2):
+        sends.arrived(rows_tile.at[way, corner_rows, own_cols], gcorner_sem.at[way], corners[way])
+    corner = rows_tile.at[:, corner_rows, own_cols]
+    sends.start(corner, corner, gsibhalo_sem.at[7], sibling)
+    for slot in range(8):
+        distance = BLOCKS[slot]
+        sends.arrived(
+            rows_tile.at[:, halo_place(zs[distance], 1 - c), columns_of(distance)], gsibhalo_sem.at[slot], sibling
+        )
+    for copy in locals_[1:]:
+        copy.wait()
+    narrow(slice(0, HALO))
+    narrow(slice(HALO + 256, 512))
+    for plane in range(2):
+        patch[FRAME * plane : FRAME * (plane + 1)] = dot(lines, narrowed[plane, 0]) + dot(lines, narrowed[plane, 1])
 
     pr, pi = patch[:FRAME], patch[FRAME:]
     for k in range(MODES):
@@ -318,7 +334,7 @@
         )
 
     def first_copy(k, i):
-        h = k // 2
+        h = k % 2
         tx, ty = (x + i * h) % NX, (y + i * (1 - h)) % NY
         q = h * tx + (1 - h) * ty
         return pltpu.make_async_remote_copy(
@@ -347,32 +363,133 @@
         if k > 0:
             take_part(k - 1)
 
+    def ways(k):
+        if k % 2 == 0:
+            return y, ys, y_peer, x, xs, x_peer
+        return x, xs, x_peer, y, ys, y_peer
+
+    def second_stage(k):
+        first, _, _, _, theirs, peers = ways(k)
+        rows = pl.ds(pl.multiple_of(64 * first, 64), 64)
+        for i in range(1, 4):
+            first_copy(k, i).wait_recv()
+        sum1[k] = part[k, rows] + in1[k, 0] + in1[k, 1] + in1[k, 2]
+        for i in range(1, 4):
+            sends.start(
+                sum1.at[k, pl.ds(pl.multiple_of(16 * theirs[i], 16), 16)],
+                in2.at[k, i - 1], sem2.at[k, i - 1], peers[i],
+            )
+
+    def z_tile(pair, v):
+        return (
+            2 * pair + v // 4,
+            pl.ds(pl.multiple_of(8 * ((v // 2) % 2), 8), 8),
+            pl.ds(pl.multiple_of(128 * (v % 2), 128), 128),
+        )
+
+    def third_send(pair):
+        for k in (2 * pair, 2 * pair + 1):
+            _, _, _, second, _, peers = ways(k)
+            for i in range(1, 4):
+                sends.arrived(in2.at[k, i - 1], sem2.at[k, i - 1], peers[4 - i])
+            rows = pl.ds(pl.multiple_of(16 * second, 16), 16)
+            sum2[k] = sum1[k, rows] + in2[k, 0] + in2[k, 1] + in2[k, 2]
+        for i in range(1, 8):
+            sends.start(sum2.at[z_tile(pair, zs[i])], in3.at[pair, i - 1], sem3.at[pair, i - 1], z_peer[i])
+
+    def third_sum(pair):
+        for i in range(1, 8):
+            sends.arrived(in3.at[pair, i - 1], sem3.at[pair, i - 1], z_peer[8 - i])
+        whole = sum2[z_tile(pair, z)]
+        for i in range(1, 8):
+            whole = whole + in3[pair, i - 1]
+        all3[z_tile(pair, z)] = whole
+        for i in range(1, 8):
+            ref = all3.at[z_tile(pair, z)]
+            sends.start(ref, ref, asem3.at[pair, i - 1], z_peer[i])
+
+    def out_rows(first, second, count):
+        return pl.ds(pl.multiple_of(64 * first + 16 * second, 16), count)
+
+    def back_second(pair):
+        for i in range(1, 8):
+            sends.arrived(all3.at[z_tile(pair, zs[8 - i])], asem3.at[pair, i - 1], z_peer[8 - i])
+        for k in (2 * pair, 2 * pair + 1):
+            first, _, _, second, _, peers = ways(k)
+            rows = out_rows(first, second, 16)
+            for i in range(1, 4):
+                sends.start(all3.at[k], probe_out.at[c, k, rows], asem2.at[k, i - 1], peers[i])
+            probe_out[c, k, rows] = all3[k]
+
+    def back_first(pair):
+        for k in (2 * pair, 2 * pair + 1):
+            first, _, first_peers, _, theirs, peers = ways(k)
+            for i in range(1, 4):
+                ref = probe_out.at[c, k, out_rows(first, theirs[4 - i], 16)]
+                sends.arrived(ref, asem2.at[k, i - 1], peers[4 - i])
+            ref = probe_out.at[c, k, out_rows(first, 0, 64)]
+            for i in range(1, 4):
+                sends.start(ref, ref, asem1.at[k, i - 1], first_peers[i])
+            sends.start(ref, ref, asem0.at[k, 0], sibling)
+
+    def hand_over(pair):
+        for k in (2 * pair, 2 * pair + 1):
+            _, theirs, peers, _, _, _ = ways(k)
+            for i in range(1, 4):
+                ref = probe_out.at[c, k, out_rows(theirs[4 - i], 0, 64)]
+                sends.arrived(ref, asem1.at[k, i - 1], peers[4 - i])
+                sends.start(ref, ref, asem0.at[k, i], sibling)
+
     columns_back = one_hot((FRAME, 640), lambda i, j: j == i + c0)
 
-    def put(core, dst):
-        lines_back = one_hot(
-            (FRAME, FRAME), lambda i, j: 64 * (i // STRIP) + STRIP * core + i % STRIP == j + r0
-        )
+    gradient_parts = split(jnp.concatenate([grad[0], grad[1]], axis=1))
+
+    def put(core, dst, rims):
+        strips = (0, 1, 6, 7) if rims else (2, 3, 4, 5)
+
+        def hit(i, j):
+            q = i // STRIP
+            strip = q + 4 * (q // 2) if rims else q + 2
+            return 64 * strip + STRIP * core + i % STRIP == j + r0
+
+        lines_back = one_hot((128, FRAME), hit)
+        found = 0.0
+        for value in gradient_parts:
+            rows = dot(lines_back, value).astype(bf16)
+            found = found + dot(jnp.concatenate([rows[:, :FRAME], rows[:, FRAME:]], axis=0), columns_back)
         for plane in range(2):
-            found = pick_columns(pick_rows(lines_back, grad[plane]), columns_back)
-            for j in range(8):
-                dst[j, plane] = found[STRIP * j : STRIP * (j + 1)]
-
-    put(1 - c, sib_out)
-    for k in (0, 3, 1, 2):
+            for q in range(4):
+                dst[strips[q], plane] = found[128 * plane + STRIP * q : 128 * plane + STRIP * (q + 1)]
+
+    def sib_send(k):
         both = pl.ds(2 * k, 2)
         sends.start(sib_out.at[both], sib_in.at[both], sib_sem.at[k], sibling)
-    put(c, total)
-    take_part(3)
-    early = zh % 2
-    for k in (0, 3, 1, 2):
+
+    def sib_add(k):
         both = pl.ds(2 * k, 2)
         sends.arrived(sib_in.at[both], sib_sem.at[k], sibling)
         total[both] += sib_in[both]
-        if k == 3:
-            for i in (early, 1 - early):
-                sends.start(total.at[i], halo_in.at[0, i], halo_sem.at[0, i], wide_down)
-                sends.start(total.at[6 + i], halo_in.at[1, i], halo_sem.at[1, i], wide_up)
+
+    early = zh % 2
+    put(1 - c, sib_out, True)
+    sib_send(0)
+    sib_send(3)
+    second_stage(0)
+    put(c, total, True)
+    put(1 - c, sib_out, False)
+    sib_send(1)
+    sib_send(2)
+    sib_add(0)
+    sib_add(3)
+    for i in (early, 1 - early):
+        sends.start(total.at[i], halo_in.at[0, i], halo_sem.at[0, i], wide_down)
+        sends.start(total.at[6 + i], halo_in.at[1, i], halo_sem.at[1, i], wide_up)
+    take_part(3)
+    second_stage(1)
+    put(c, total, False)
+    sib_add(1)
+    sib_add(2)
+    third_send(0)
 
     weight[...] = jnp.zeros_like(weight)
 
@@ -411,103 +528,42 @@
     def block(zb):
         return total.at[2 + zb // 2, :, :, own_cols]
 
-    def second_stage(half):
-        first = (y if half == 0 else x)
-        peers = (y_peer if half == 0 else x_peer)
-        rows = pl.ds(pl.multiple_of(64 * first, 64), 64)
-        for k in (2 * half, 2 * half + 1):
-            for i in range(1, 4):
-                first_copy(k, i).wait_recv()
-            sum1[k] = part[k, rows] + in1[k, 0] + in1[k, 1] + in1[k, 2]
-        both = pl.ds(2 * half, 2)
-        for i in range(1, 4):
-            q = (xs if half == 0 else ys)[i]
+    second_stage(2)
+    second_stage(3)
+    take_halo(early)
+    for way in range(2):
+        sends.start(block(zs[4]).at[way], in_four.at[way], four_sem.at[way], onward[way])
+    third_sum(0)
+    third_send(1)
+    take_halo(1 - early)
+    for way in range(2):
+        for step in range(2):
+            distance = ((1, 3), (7, 5))[way][step]
             sends.start(
-                sum1.at[both, pl.ds(pl.multiple_of(16 * q, 16), 16)],
-                in2.at[half, i - 1], sem2.at[half, i - 1],
-                (x_peer if half == 0 else y_peer)[i],
+                total.at[2 + zs[distance] // 2, :, :, side_cols], in_side.at[way, step], side_sem.at[way, step],
+                near_peer[way],
             )
-
-    second_stage(0)
-    second_stage(1)
-    take_halo(early)
-    for way in range(2):
-        sends.start(block(zs[4]).at[way], in_four.at[way], four_sem.at[way], onward[way])
-
-    for half in range(2):
-        second = (x if half == 0 else y)
-        peers = (x_peer if half == 0 else y_peer)
-        for i in range(1, 4):
-            sends.arrived(in2.at[half, i - 1], sem2.at[half, i - 1], peers[4 - i])
-        rows = pl.ds(pl.multiple_of(16 * second, 16), 16)
-        both = pl.ds(2 * half, 2)
-        sum2[both] = sum1[both, rows] + in2[half, 0] + in2[half, 1] + in2[half, 2]
-
-    def z_tile(v):
-        return (
-            pl.ds(2 * (v // 4), 2),
-            pl.ds(pl.multiple_of(8 * ((v // 2) % 2), 8), 8),
-            pl.ds(pl.multiple_of(128 * (v % 2), 128), 128),
-        )
-
-    for i in range(1, 8):
-        sends.start(sum2.at[z_tile(zs[i])], in3.at[i - 1], sem3.at[i - 1], z_peer[i])
-    take_halo(1 - early)
-    for way in range(2):
-        sends.start(
-            block(zs[2 if way == 0 else 6]).at[1 - way], in_two.at[way, 1 - way], two_sem.at[way, 1 - way], onward[way]
-        )
-    for i, distance in enumerate((1, 7, 3, 5)):
-        sends.start(
-            total.at[2 + zs[distance] // 2, :, :, side_cols], in_side.at[i], side_sem.at[i], z_peer[distance]
-        )
     lamp(0)
     sends.arrived(where.at[2], where_sem.at[9], wide_up)
-    for i in range(1, 8):
-        sends.arrived(in3.at[i - 1], sem3.at[i - 1], z_peer[8 - i])
-    whole = sum2[z_tile(z)]
-    for i in range(1, 8):
-        whole = whole + in3[i - 1]
-    all3[z_tile(z)] = whole
-    for i in range(1, 8):
-        ref = all3.at[z_tile(z)]
-        sends.start(ref, ref, asem3.at[i - 1], z_peer[i])
+    near = pl.ds(pl.multiple_of(384 - 256 * m, 128), 128)
+    for way in range(2):
+        sends.arrived(in_side.at[way, 1], side_sem.at[way, 1], near_peer[1 - way])
+        zb = zs[2 if way == 0 else 6]
+        total[2 + zb // 2, :, :, near] += in_side[way, 1]
+        sends.start(block(zb).at[1 - way], in_two.at[way, 1 - way], two_sem.at[way, 1 - way], onward[way])
     for way in range(2):
         sends.arrived(in_four.at[way], four_sem.at[way], behind[way])
         in_four[way] += block(zs[2 if way == 0 else 6])[way]
         sends.start(in_four.at[way], in_two.at[way, way], two_sem.at[way, way], onward[way])
-
-    for i in range(1, 8):
-        sends.arrived(all3.at[z_tile(zs[8 - i])], asem3.at[i - 1], z_peer[8 - i])
-    for half in range(2):
-        second = (x if half == 0 else y)
-        peers = (x_peer if half == 0 else y_peer)
-        rows = pl.ds(pl.multiple_of(16 * second, 16), 16)
-        both = pl.ds(2 * half, 2)
-        all2[both, rows] = all3[both]
-        for i in range(1, 4):
-            sends.start(all3.at[both], all2.at[both, rows], asem2.at[half, i - 1], peers[i])
-
+    back_second(0)
+    third_sum(1)
     lamp(2)
-    for half in range(2):
-        theirs = (xs if half == 0 else ys)
-        peers = (x_peer if half == 0 else y_peer)
-        both = pl.ds(2 * half, 2)
-        for i in range(1, 4):
-            rows = pl.ds(pl.multiple_of(16 * theirs[4 - i], 16), 16)
-            sends.arrived(all2.at[both, rows], asem2.at[half, i - 1], peers[4 - i])
-        first = (y if half == 0 else x)
-        peers = (y_peer if half == 0 else x_peer)
-        rows = pl.ds(pl.multiple_of(64 * first, 64), 64)
-        for i in range(1, 4):
-            sends.start(all2.at[both], probe_out.at[c, both, rows], asem1.at[half, i - 1], peers[i])
-        sends.start(all2.at[both], probe_out.at[c, both, rows], asem0.at[half, 0], sibling)
-        probe_out[c, both, rows] = all2[both]
-
-    near = pl.ds(pl.multiple_of(384 - 256 * m, 128), 128)
-    for i, distance in enumerate((7, 1, 5, 3)):
-        sends.arrived(in_side.at[i], side_sem.at[i], z_peer[distance])
-    total[2 + zh, :, :, near] += in_side[0] + in_side[1] + in_side[2] + in_side[3]
+    back_first(0)
+    back_second(1)
+
+    for way in range(2):
+        sends.arrived(in_side.at[way, 0], side_sem.at[way, 0], near_peer[1 - way])
+    total[2 + zh, :, :, near] += in_side[0, 0] + in_side[1, 0]
     for way in range(2):
         for plane in range(2):
             sends.arrived(in_two.at[way, plane], two_sem.at[way, plane], behind[way])
@@ -539,32 +595,34 @@
     tile_send(0, [None, sibling], 0)
     tile_sum(0, [None, sibling], 0)
     tile_send(1, plane_peer, 1)
+    back_first(1)
+    hand_over(0)
     tile_sum(1, plane_peer, 1)
     tile_send(2, z_peer, 16)
+    hand_over(1)
     tile_sum(2, z_peer, 16)
     sums = tile[3]
     alpha = sums[0:1, 0:1] / sums[1:2, 0:1]
     step_out[...] = direction[...] * alpha
-    for half in range(2):
-        theirs = (ys if half == 0 else xs)
-        peers = (y_peer if half == 0 else x_peer)
-        both = pl.ds(2 * half, 2)
-        for i in range(1, 4):
-            rows = pl.ds(pl.multiple_of(64 * theirs[4 - i], 64), 64)
-            ref = probe_out.at[c, both, rows]
-            sends.arrived(ref, asem1.at[half, i - 1], peers[4 - i])
-            sends.start(ref, ref, asem0.at[half, i], sibling)
-    for half in range(2):
-        theirs = (ys if half == 0 else xs)
-        both = pl.ds(2 * half, 2)
+    for k in range(MODES):
+        _, theirs, _, _, _, _ = ways(k)
         for i in range(4):
-            rows = pl.ds(pl.multiple_of(64 * theirs[(4 - i) % 4], 64), 64)
-            sends.arrived(probe_out.at[1 - c, both, rows], asem0.at[half, i], sibling)
+            sends.arrived(probe_out.at[1 - c, k, out_rows(theirs[(4 - i) % 4], 0, 64)], asem0.at[k, i], sibling)
     for k in range(MODES):
         part_copy(k).wait_send()
         for i in range(1, 4):
             first_copy(k, i).wait_send()
     sends.finish()
+
+
+def hand_out_kernel(step_in, probe_in, step_out, probe_out, sem):
+    copies = [pltpu.make_async_copy(step_in, step_out, sem.at[0])]
+    for plane in range(2):
+        copies.append(pltpu.make_async_copy(probe_in.at[plane], probe_out.at[plane], sem.at[1 + plane]))
+    for copy in copies:
+        copy.start()
+    for copy in copies:
+        copy.wait()
 
 
 VMEM = pl.BlockSpec(memory_space=pltpu.VMEM)
@@ -588,6 +646,7 @@
             v(2, MODES, FRAME, FRAME),
             v(FRAME, FRAME),
             pltpu.VMEM((6, FRAME, FRAME), bf16),
+            pltpu.VMEM((2, 2, 512, FRAME), bf16),
             v(MODES + 1, 512, FRAME),
             v(FRAME, FRAME),
             v(FRAME, FRAME),
@@ -599,7 +658,7 @@
             v(2, 2, 2, STRIP, 640),
             v(2, STRIP, 512),
             v(2, 2, STRIP, 512),
-            v(4, 2, STRIP, 128),
+            v(2, 2, 2, STRIP, 128),
             v(STRIP, 512),
             v(2, STRIP, 512),
             pltpu.VMEM((16, 2, STRIP, FRAME), bf16),
@@ -608,16 +667,16 @@
             v(MODES, FRAME, FRAME),
             v(MODES, 3, 64, FRAME),
             v(MODES, 64, FRAME),
-            v(2, 3, 2, 16, FRAME),
+            v(MODES, 3, 16, FRAME),
             v(MODES, 16, FRAME),
-            v(7, 2, 8, 128),
+            v(2, 7, 8, 128),
             v(MODES, 16, FRAME),
-            v(MODES, 64, FRAME),
             v(4, 8, 128),
             v(23, 8, 128),
             DMA((N_SENDS,)),
             DMA((4,)),
             DMA((2, 2)),
+            DMA((2,)),
             DMA((2,)),
             DMA((2, 2)),
             DMA((8,)),
@@ -628,17 +687,17 @@
             DMA((2, 2)),
             DMA((2,)),
             DMA((2, 2)),
-            DMA((4,)),
+            DMA((2, 2)),
             DMA((MODES,)),
             DMA((MODES,)),
             DMA((MODES, 3)),
             DMA((MODES, 3)),
-            DMA((2, 3)),
-            DMA((7,)),
-            DMA((7,)),
-            DMA((2, 3)),
-            DMA((2, 3)),
-            DMA((2, 4)),
+            DMA((MODES, 3)),
+            DMA((2, 7)),
+            DMA((2, 7)),
+            DMA((MODES, 3)),
+            DMA((MODES, 3)),
+            DMA((MODES, 4)),
             DMA((23,)),
         ],
         compiler_params=pltpu.CompilerParams(
@@ -647,11 +706,21 @@
     )(obj, probe, amp, tables, row, col)
 
 
+def hand_out(step, gradient):
+    return pl.pallas_call(
+        hand_out_kernel,
+        out_shape=[jax.ShapeDtypeStruct(step.shape, f32), jax.ShapeDtypeStruct(gradient.shape, f32)],
+        in_specs=[ANY, ANY],
+        out_specs=[ANY, ANY],
+        scratch_shapes=[DMA((3,))],
+    )(step, gradient)
+
+
 def per_device(obj_tile, probe, amplitude, row_offsets, col_offsets):
     step, gradient = update(
         obj_tile, probe, amplitude.reshape((FRAME, FRAME)), jnp.asarray(dft_tables()), row_offsets, col_offsets
     )
-    return step, gradient
+    return hand_out(step, gradient)
 
 
 def solution(mesh):

time: 98.5 us -> 162 us (1.64)
  Pallas kernels: 94.5 us -> 158 us
    pallas_call x0 -> x1, Pallas kernels: none -> 68.6 us  [hand_out(): pl.pallas_call(hand_out_kernel, out_shape=[jax.ShapeDtypeStruct(step.shap...]
    pallas_call x1, Pallas kernels: 94.5 us -> 89.7 us  [update(): pl.pallas_call(update_kernel, out_shape=[pltpu.VMEM((2, STRIP, 512), f32)...]
where the time goes in v4:
time: 162 us
  Pallas kernels  158 us (98%)
  local copies, waits for them, and re-layouts  2 us (1%)
  between operations  1.94 us (1%)
    pallas_call x1, Pallas kernels, update(): pl.pallas_call(update_kernel, out_shape=[pltpu.VMEM((2, STRIP, 512), f32)...  89.7 us
    pallas_call x1, Pallas kernels, hand_out(): pl.pallas_call(hand_out_kernel, out_shape=[jax.ShapeDtypeStruct(step.shap...  68.6 us

profile of v4, /device:TPU:1, one launch (start us, length us, event | category | flops | bytes accessed | tf_op | source)
XLA Modules:
  0.0 162.3 jit_solution(17738275453188030765)
XLA Ops:
  1.9 89.7 %shard_map.77 = (f32[2,32,512]{2,1,0:T(8,128)S(1)}, f32[2,4,256,256]{3,2,1,0:T(8,128)S(1)}) custom-call(f32[2,32,512]{2,1,0:T(8,128)} %obj.1, f32[2,4,256,256]{3,2,1,0:T(8,128)} %probe_in.1, f32[256,256]{1,0:T(8,128)} %bitcast.1, bf16[6,256,256]{2,1,0:T(8,128)(2,1)} %constant.2.clone.tables_in, s32[1,1,1]{2,1,0:T(1,128)S(6)} %copy.8.row_in, ...), custom_call_target="tpu_custom_call" | custom-call | tf_op jit(solution)/shard_map/pallas_call | solution.py:636
  91.7 0.0 copy-start
  91.7 1.3 copy-done
  93.0 0.0 copy-start.1
  93.0 0.7 copy-done.1
  93.7 68.6 %shard_map.78 = (f32[2,32,512]{2,1,0:T(8,128)}, f32[2,4,256,256]{3,2,1,0:T(8,128)}) custom-call(f32[2,32,512]{2,1,0:T(8,128)} %copy-done.1, f32[2,4,256,256]{3,2,1,0:T(8,128)} %copy-done), custom_call_target="tpu_custom_call" | custom-call | tf_op jit(solution)/shard_map/pallas_call | solution.py:710
Async XLA Ops:
  91.7 1.3 copy-start
  93.0 0.7 copy-start.1

commit v5 on v4

--- a/solution.py
+++ b/solution.py
@@ -37,6 +37,7 @@
     def __init__(self, sem):
         self.sem = sem
         self.copies = []
+        self.waited = 0
 
     def start(self, src, dst, recv_sem, target):
         copy = pltpu.make_async_remote_copy(
@@ -60,9 +61,16 @@
             device_id_type=MESH,
         ).wait_recv()
 
+    def drain(self, count):
+        for copy in self.copies[self.waited : count]:
+            copy.wait_send()
+        self.waited = max(self.waited, count)
+
+    def mark(self):
+        return len(self.copies)
+
     def finish(self):
-        for copy in self.copies:
-            copy.wait_send()
+        self.drain(len(self.copies))
 
 
 def greet(peers):
@@ -125,14 +133,24 @@
     return jnp.where(hit(lax.broadcasted_iota(jnp.int32, shape, 0), lax.broadcasted_iota(jnp.int32, shape, 1)), 1.0, 0.0).astype(bf16)
 
 
+def pick_columns(x, table):
+    high, low = split(x)
+    return dot(high, table) + dot(low, table)
+
+
+def pick_rows(table, x):
+    high, low = split(x)
+    return dot(table, high) + dot(table, low)
+
+
 def update_kernel(
     obj, probe_in, amp_in, tables_in, row_in, col_in,
     step_out, probe_out,
     rows_tile, probe, amp, tables, narrowed, far, factor, light, grad, where,
-    sib_out, sib_in, total, halo_in, in_four, in_two, in_side, weight, direction, lit,
+    sib_out, sib_in, total, halo_in, in_four, in_two, in_side, in_far, weight, direction, lit,
     probe_part, part_in, part, in1, sum1, in2, sum2, in3, all3, tile, tiles_in,
-    send_sem, local_sem, gtwo_sem, gfour_sem, gcorner_sem, gside_sem, gsib_sem, ghalo_sem, gsibhalo_sem, where_sem,
-    sib_sem, halo_sem, four_sem, two_sem, side_sem, part_sem, part_send_sem, sem1, send1_sem, sem2, sem3,
+    send_sem, local_sem, gtwo_sem, gfour_sem, gside_sem, gsib_sem, ghalo_sem, gsibhalo_sem, where_sem,
+    sib_sem, halo_sem, four_sem, two_sem, side_sem, far_sem, part_sem, part_send_sem, sem1, send1_sem, sem2, sem3,
     asem3, asem2, asem1, asem0, tile_sem,
 ):
     x, y, z, c = here()
@@ -154,6 +172,8 @@
     near_peer = (z_peer[1], z_peer[7])
     sends = Sends(send_sem)
 
+    everyone = [sibling] + plane_peer[1:] + z_peer[1:]
+    greet(everyone)
     locals_ = [
         pltpu.make_async_copy(a, b, local_sem.at[i])
         for i, (a, b) in enumerate(
@@ -167,19 +187,6 @@
     c0 = offset_col - HALO * (1 - m)
     lane = lax.broadcasted_iota(jnp.int32, (1, 128), 1)
     where[1, 8 * c + z] = jnp.where(lane == 0, r0, offset_col)
-    def beside(row_tile, way):
-        return (row_tile % ROW_TILES, m, (zs[2 if way == 0 else 6] // 2) * 2 + c)
-
-    corners = [beside(w + 1, 0), beside(w + 1, 1), beside(w + ROW_TILES - 1, 0), beside(w + ROW_TILES - 1, 1)]
-    everyone = [sibling] + plane_peer[1:] + z_peer[1:] + corners
-    greet(everyone)
-    locals_[0].wait()
-    light[...] = jnp.zeros_like(light)
-
-    @pl.loop(0, MODES)
-    def _(k):
-        light[...] += probe[0, k] * probe[0, k] + probe[1, k] * probe[1, k]
-
     met(everyone)
 
     def strip_of(zb, core):
@@ -197,20 +204,17 @@
     def halo_place(zb, core):
         s = strip_of(zb, core)
         return pl.ds(pl.multiple_of(HALO + STRIP * s + 256 * (1 - 2 * (s // 4)), STRIP), STRIP)
-
-    def towards(zb):
-        return (w + ROW_TILES + 2 * (strip_of(zb, c) // 4) - 1) % ROW_TILES
 
     def pass_on(slot, src=None):
         distance = BLOCKS[slot]
         zb = zs[distance]
         cols = columns_of(distance)
         ref = rows_tile.at[:, place(zb, c), cols]
-        if distance != 4:
-            sends.start(
-                ref if src is None else src,
-                rows_tile.at[:, halo_place(zb, c), cols], ghalo_sem.at[slot], (towards(zb), m, n),
-            )
+        towards = (w + ROW_TILES + 2 * (strip_of(zb, c) // 4) - 1) % ROW_TILES
+        sends.start(
+            ref if src is None else src,
+            rows_tile.at[:, halo_place(zb, c), cols], ghalo_sem.at[slot], (towards, m, n),
+        )
         sends.start(ref if src is None else src, ref, gsib_sem.at[slot], sibling)
 
     mine = where.at[1, pl.ds(8 * c + z, 1)]
@@ -232,17 +236,18 @@
         sends.start(obj.at[:, :, out_cols], rows_tile.at[:, rows, there], gside_sem.at[way, 0], near_peer[way])
     own = pltpu.make_async_copy(obj, rows_tile.at[:, rows, own_cols], local_sem.at[3])
     own.start()
+    locals_[0].wait()
+    light[...] = jnp.zeros_like(light)
+
+    @pl.loop(0, MODES)
+    def _(k):
+        light[...] += probe[0, k] * probe[0, k] + probe[1, k] * probe[1, k]
+
     for way in range(2):
         zb = zs[6 if way == 0 else 2]
         ref = rows_tile.at[way, place(zb, c), own_cols]
         sends.arrived(ref, gtwo_sem.at[way, way], behind[way])
         sends.start(ref, ref, gfour_sem.at[way], onward[way])
-    for way in range(2):
-        zb = zs[6 if way == 0 else 2]
-        sends.start(
-            rows_tile.at[way, place(zb, c), own_cols], rows_tile.at[way, halo_place(zb, c), own_cols],
-            gcorner_sem.at[way], beside(towards(zb), way),
-        )
     for way in range(2):
         zb = zs[6 if way == 0 else 2]
         sends.arrived(rows_tile.at[1 - way, place(zb, c), own_cols], gtwo_sem.at[way, 1 - way], behind[way])
@@ -298,11 +303,7 @@
                 narrowed[plane, part, rows] = dot(value, columns).astype(bf16)
 
     narrow(slice(HALO, HALO + 256))
-    corner_rows = halo_place(zs[4], c)
-    for way in range(2):
-        sends.arrived(rows_tile.at[way, corner_rows, own_cols], gcorner_sem.at[way], corners[way])
-    corner = rows_tile.at[:, corner_rows, own_cols]
-    sends.start(corner, corner, gsibhalo_sem.at[7], sibling)
+    halo_arrived(7)
     for slot in range(8):
         distance = BLOCKS[slot]
         sends.arrived(
@@ -442,54 +443,33 @@
 
     columns_back = one_hot((FRAME, 640), lambda i, j: j == i + c0)
 
-    gradient_parts = split(jnp.concatenate([grad[0], grad[1]], axis=1))
-
-    def put(core, dst, rims):
-        strips = (0, 1, 6, 7) if rims else (2, 3, 4, 5)
-
-        def hit(i, j):
-            q = i // STRIP
-            strip = q + 4 * (q // 2) if rims else q + 2
-            return 64 * strip + STRIP * core + i % STRIP == j + r0
-
-        lines_back = one_hot((128, FRAME), hit)
-        found = 0.0
-        for value in gradient_parts:
-            rows = dot(lines_back, value).astype(bf16)
-            found = found + dot(jnp.concatenate([rows[:, :FRAME], rows[:, FRAME:]], axis=0), columns_back)
+    def put(core, dst):
+        lines_back = one_hot(
+            (FRAME, FRAME), lambda i, j: 64 * (i // STRIP) + STRIP * core + i % STRIP == j + r0
+        )
         for plane in range(2):
-            for q in range(4):
-                dst[strips[q], plane] = found[128 * plane + STRIP * q : 128 * plane + STRIP * (q + 1)]
-
-    def sib_send(k):
+            found = pick_columns(pick_rows(lines_back, grad[plane]), columns_back)
+            for j in range(8):
+                dst[j, plane] = found[STRIP * j : STRIP * (j + 1)]
+
+    gathered = sends.mark()
+    put(1 - c, sib_out)
+    for k in (0, 3, 1, 2):
         both = pl.ds(2 * k, 2)
         sends.start(sib_out.at[both], sib_in.at[both], sib_sem.at[k], sibling)
-
-    def sib_add(k):
+    take_part(3)
+    put(c, total)
+    second_stage(0)
+    early = zh % 2
+    for k in (0, 3, 1, 2):
         both = pl.ds(2 * k, 2)
         sends.arrived(sib_in.at[both], sib_sem.at[k], sibling)
         total[both] += sib_in[both]
-
-    early = zh % 2
-    put(1 - c, sib_out, True)
-    sib_send(0)
-    sib_send(3)
-    second_stage(0)
-    put(c, total, True)
-    put(1 - c, sib_out, False)
-    sib_send(1)
-    sib_send(2)
-    sib_add(0)
-    sib_add(3)
-    for i in (early, 1 - early):
-        sends.start(total.at[i], halo_in.at[0, i], halo_sem.at[0, i], wide_down)
-        sends.start(total.at[6 + i], halo_in.at[1, i], halo_sem.at[1, i], wide_up)
-    take_part(3)
+        if k == 3:
+            for i in (early, 1 - early):
+                sends.start(total.at[i], halo_in.at[0, i], halo_sem.at[0, i], wide_down)
+                sends.start(total.at[6 + i], halo_in.at[1, i], halo_sem.at[1, i], wide_up)
     second_stage(1)
-    put(c, total, False)
-    sib_add(1)
-    sib_add(2)
-    third_send(0)
 
     weight[...] = jnp.zeros_like(weight)
 
@@ -518,6 +498,7 @@
 
     lamp(1)
     sends.arrived(where.at[0], where_sem.at[8], wide_down)
+    sends.drain(gathered)
 
     def take_halo(i):
         for side in range(2):
@@ -530,40 +511,50 @@
 
     second_stage(2)
     second_stage(3)
+    third_send(0)
     take_halo(early)
     for way in range(2):
         sends.start(block(zs[4]).at[way], in_four.at[way], four_sem.at[way], onward[way])
-    third_sum(0)
     third_send(1)
     take_halo(1 - early)
     for way in range(2):
-        for step in range(2):
-            distance = ((1, 3), (7, 5))[way][step]
-            sends.start(
-                total.at[2 + zs[distance] // 2, :, :, side_cols], in_side.at[way, step], side_sem.at[way, step],
-                near_peer[way],
-            )
+        zb = zs[2 if way == 0 else 6]
+        sends.start(block(zb).at[1 - way], in_two.at[way, 1 - way], two_sem.at[way, 1 - way], onward[way])
+    for way in range(2):
+        distance, beyond = ((1, 3), (7, 5))[way]
+        sends.start(
+            total.at[2 + zs[beyond] // 2, way, :, side_cols], in_far.at[way, 0], far_sem.at[way, 0], near_peer[way]
+        )
+        sends.start(
+            total.at[2 + zs[distance] // 2, :, :, side_cols], in_side.at[way], side_sem.at[way], near_peer[way]
+        )
+        sends.start(
+            total.at[2 + zs[beyond] // 2, 1 - way, :, side_cols], in_far.at[way, 1], far_sem.at[way, 1], z_peer[beyond]
+        )
+    third_sum(0)
     lamp(0)
     sends.arrived(where.at[2], where_sem.at[9], wide_up)
     near = pl.ds(pl.multiple_of(384 - 256 * m, 128), 128)
     for way in range(2):
-        sends.arrived(in_side.at[way, 1], side_sem.at[way, 1], near_peer[1 - way])
         zb = zs[2 if way == 0 else 6]
-        total[2 + zb // 2, :, :, near] += in_side[way, 1]
-        sends.start(block(zb).at[1 - way], in_two.at[way, 1 - way], two_sem.at[way, 1 - way], onward[way])
-    for way in range(2):
+        sends.arrived(in_far.at[way, 0], far_sem.at[way, 0], near_peer[1 - way])
+        total[2 + zb // 2, way, :, near] += in_far[way, 0]
         sends.arrived(in_four.at[way], four_sem.at[way], behind[way])
-        in_four[way] += block(zs[2 if way == 0 else 6])[way]
+        in_four[way] += block(zb)[way]
         sends.start(in_four.at[way], in_two.at[way, way], two_sem.at[way, way], onward[way])
+    scattered = sends.mark()
+    third_sum(1)
     back_second(0)
-    third_sum(1)
     lamp(2)
+    back_second(1)
     back_first(0)
-    back_second(1)
-
-    for way in range(2):
-        sends.arrived(in_side.at[way, 0], side_sem.at[way, 0], near_peer[1 - way])
-    total[2 + zh, :, :, near] += in_side[0, 0] + in_side[1, 0]
+    sends.drain(scattered)
+
+    for way in range(2):
+        sends.arrived(in_side.at[way], side_sem.at[way], near_peer[1 - way])
+        sends.arrived(in_far.at[way, 1], far_sem.at[way, 1], z_peer[5 if way == 0 else 3])
+        total[2 + zh, 1 - way, :, near] += in_far[way, 1]
+    total[2 + zh, :, :, near] += in_side[0] + in_side[1]
     for way in range(2):
         for plane in range(2):
             sends.arrived(in_two.at[way, plane], two_sem.at[way, plane], behind[way])
@@ -593,13 +584,19 @@
         tile[stage + 1] = found
 
     tile_send(0, [None, sibling], 0)
+    back_first(1)
     tile_sum(0, [None, sibling], 0)
     tile_send(1, plane_peer, 1)
-    back_first(1)
     hand_over(0)
+    for k in range(MODES):
+        part_copy(k).wait_send()
+        for i in range(1, 4):
+            first_copy(k, i).wait_send()
     tile_sum(1, plane_peer, 1)
     tile_send(2, z_peer, 16)
+    closing = sends.mark()
     hand_over(1)
+    sends.drain(closing)
     tile_sum(2, z_peer, 16)
     sums = tile[3]
     alpha = sums[0:1, 0:1] / sums[1:2, 0:1]
@@ -608,21 +605,7 @@
         _, theirs, _, _, _, _ = ways(k)
         for i in range(4):
             sends.arrived(probe_out.at[1 - c, k, out_rows(theirs[(4 - i) % 4], 0, 64)], asem0.at[k, i], sibling)
-    for k in range(MODES):
-        part_copy(k).wait_send()
-        for i in range(1, 4):
-            first_copy(k, i).wait_send()
     sends.finish()
-
-
-def hand_out_kernel(step_in, probe_in, step_out, probe_out, sem):
-    copies = [pltpu.make_async_copy(step_in, step_out, sem.at[0])]
-    for plane in range(2):
-        copies.append(pltpu.make_async_copy(probe_in.at[plane], probe_out.at[plane], sem.at[1 + plane]))
-    for copy in copies:
-        copy.start()
-    for copy in copies:
-        copy.wait()
 
 
 VMEM = pl.BlockSpec(memory_space=pltpu.VMEM)
@@ -658,7 +641,8 @@
             v(2, 2, 2, STRIP, 640),
             v(2, STRIP, 512),
             v(2, 2, STRIP, 512),
-            v(2, 2, 2, STRIP, 128),
+            v(2, 2, STRIP, 128),
+            v(2, 2, STRIP, 128),
             v(STRIP, 512),
             v(2, STRIP, 512),
             pltpu.VMEM((16, 2, STRIP, FRAME), bf16),
@@ -677,7 +661,6 @@
             DMA((4,)),
             DMA((2, 2)),
             DMA((2,)),
-            DMA((2,)),
             DMA((2, 2)),
             DMA((8,)),
             DMA((8,)),
@@ -687,6 +670,7 @@
             DMA((2, 2)),
             DMA((2,)),
             DMA((2, 2)),
+            DMA((2,)),
             DMA((2, 2)),
             DMA((MODES,)),
             DMA((MODES,)),
@@ -706,21 +690,11 @@
     )(obj, probe, amp, tables, row, col)
 
 
-def hand_out(step, gradient):
-    return pl.pallas_call(
-        hand_out_kernel,
-        out_shape=[jax.ShapeDtypeStruct(step.shape, f32), jax.ShapeDtypeStruct(gradient.shape, f32)],
-        in_specs=[ANY, ANY],
-        out_specs=[ANY, ANY],
-        scratch_shapes=[DMA((3,))],
-    )(step, gradient)
-
-
 def per_device(obj_tile, probe, amplitude, row_offsets, col_offsets):
     step, gradient = update(
         obj_tile, probe, amplitude.reshape((FRAME, FRAME)), jnp.asarray(dft_tables()), row_offsets, col_offsets
     )
-    return hand_out(step, gradient)
+    return step, gradient
 
 
 def solution(mesh):

time: 162 us -> 91.6 us (0.57)
  Pallas kernels: 158 us -> 87 us
    pallas_call x1 -> x0, Pallas kernels: 68.6 us -> none  [hand_out(): pl.pallas_call(hand_out_kernel, out_shape=[jax.ShapeDtypeStruct(step.shap...]
    pallas_call x1, Pallas kernels: 89.7 us -> 87 us  [update(): pl.pallas_call(update_kernel, out_shape=[pltpu.VMEM((2, STRIP, 512), f32)...]
where the time goes in v5:
time: 91.6 us; the launch traced here: 90.9 us
  Pallas kernels  87 us (95%)
  local copies, waits for them, and re-layouts  1.98 us (2%)
  between operations  1.93 us (2%)
    pallas_call x1, Pallas kernels, update(): pl.pallas_call(update_kernel, out_shape=[pltpu.VMEM((2, STRIP, 512), f32)...  87 us
    unnamed x2, local copies, waits for them, and re-layouts  1.98 us

profile of v5, /device:TPU:1, one launch (start us, length us, event | category | flops | bytes accessed | tf_op | source)
XLA Modules:
  0.0 90.9 jit_solution(16361178238906925364)
XLA Ops:
  1.9 87.0 %shard_map.77 = (f32[2,32,512]{2,1,0:T(8,128)S(1)}, f32[2,4,256,256]{3,2,1,0:T(8,128)S(1)}) custom-call(f32[2,32,512]{2,1,0:T(8,128)} %obj.1, f32[2,4,256,256]{3,2,1,0:T(8,128)} %probe_in.1, f32[256,256]{1,0:T(8,128)} %bitcast.1, bf16[6,256,256]{2,1,0:T(8,128)(2,1)} %constant.2.clone.tables_in, s32[1,1,1]{2,1,0:T(1,128)S(6)} %copy.12.row_in, ...), custom_call_target="tpu_custom_call" | custom-call | tf_op jit(solution)/shard_map/pallas_call | solution.py:619
  88.9 0.7 copy.10
  89.6 1.3 %copy.11 = f32[2,4,256,256]{3,2,1,0:T(8,128)} copy(f32[2,4,256,256]{3,2,1,0:T(8,128)S(1)} %get-tuple-element.3) | data formatting | bytes 4194304

commit v6 on v5

--- a/solution.py
+++ b/solution.py
@@ -66,9 +66,6 @@
             copy.wait_send()
         self.waited = max(self.waited, count)
 
-    def mark(self):
-        return len(self.copies)
-
     def finish(self):
         self.drain(len(self.copies))
 
@@ -147,10 +144,10 @@
     obj, probe_in, amp_in, tables_in, row_in, col_in,
     step_out, probe_out,
     rows_tile, probe, amp, tables, narrowed, far, factor, light, grad, where,
-    sib_out, sib_in, total, halo_in, in_four, in_two, in_side, in_far, weight, direction, lit,
+    sib_out, sib_in, total, halo_in, in_four, in_two, in_side, weight, direction, lit,
     probe_part, part_in, part, in1, sum1, in2, sum2, in3, all3, tile, tiles_in,
     send_sem, local_sem, gtwo_sem, gfour_sem, gside_sem, gsib_sem, ghalo_sem, gsibhalo_sem, where_sem,
-    sib_sem, halo_sem, four_sem, two_sem, side_sem, far_sem, part_sem, part_send_sem, sem1, send1_sem, sem2, sem3,
+    sib_sem, halo_sem, four_sem, two_sem, side_sem, part_sem, part_send_sem, sem1, send1_sem, sem2, sem3,
     asem3, asem2, asem1, asem0, tile_sem,
 ):
     x, y, z, c = here()
@@ -172,8 +169,6 @@
     near_peer = (z_peer[1], z_peer[7])
     sends = Sends(send_sem)
 
-    everyone = [sibling] + plane_peer[1:] + z_peer[1:]
-    greet(everyone)
     locals_ = [
         pltpu.make_async_copy(a, b, local_sem.at[i])
         for i, (a, b) in enumerate(
@@ -187,6 +182,8 @@
     c0 = offset_col - HALO * (1 - m)
     lane = lax.broadcasted_iota(jnp.int32, (1, 128), 1)
     where[1, 8 * c + z] = jnp.where(lane == 0, r0, offset_col)
+    everyone = [sibling] + plane_peer[1:] + z_peer[1:]
+    greet(everyone)
     met(everyone)
 
     def strip_of(zb, core):
@@ -236,13 +233,6 @@
         sends.start(obj.at[:, :, out_cols], rows_tile.at[:, rows, there], gside_sem.at[way, 0], near_peer[way])
     own = pltpu.make_async_copy(obj, rows_tile.at[:, rows, own_cols], local_sem.at[3])
     own.start()
-    locals_[0].wait()
-    light[...] = jnp.zeros_like(light)
-
-    @pl.loop(0, MODES)
-    def _(k):
-        light[...] += probe[0, k] * probe[0, k] + probe[1, k] * probe[1, k]
-
     for way in range(2):
         zb = zs[6 if way == 0 else 2]
         ref = rows_tile.at[way, place(zb, c), own_cols]
@@ -301,6 +291,13 @@
         for plane in range(2):
             for part, value in enumerate(split(rows_tile[plane, rows])):
                 narrowed[plane, part, rows] = dot(value, columns).astype(bf16)
+
+    locals_[0].wait()
+    light[...] = jnp.zeros_like(light)
+
+    @pl.loop(0, MODES)
+    def _(k):
+        light[...] += probe[0, k] * probe[0, k] + probe[1, k] * probe[1, k]
 
     narrow(slice(HALO, HALO + 256))
     halo_arrived(7)
@@ -452,14 +449,15 @@
             for j in range(8):
                 dst[j, plane] = found[STRIP * j : STRIP * (j + 1)]
 
-    gathered = sends.mark()
+    gathered = len(sends.copies)
+    second_stage(0)
     put(1 - c, sib_out)
     for k in (0, 3, 1, 2):
         both = pl.ds(2 * k, 2)
         sends.start(sib_out.at[both], sib_in.at[both], sib_sem.at[k], sibling)
     take_part(3)
+    second_stage(1)
     put(c, total)
-    second_stage(0)
     early = zh % 2
     for k in (0, 3, 1, 2):
         both = pl.ds(2 * k, 2)
@@ -469,7 +467,7 @@
             for i in (early, 1 - early):
                 sends.start(total.at[i], halo_in.at[0, i], halo_sem.at[0, i], wide_down)
                 sends.start(total.at[6 + i], halo_in.at[1, i], halo_sem.at[1, i], wide_up)
-    second_stage(1)
+    third_send(0)
 
     weight[...] = jnp.zeros_like(weight)
 
@@ -498,7 +496,6 @@
 
     lamp(1)
     sends.arrived(where.at[0], where_sem.at[8], wide_down)
-    sends.drain(gathered)
 
     def take_halo(i):
         for side in range(2):
@@ -511,50 +508,43 @@
 
     second_stage(2)
     second_stage(3)
-    third_send(0)
+    sends.drain(gathered)
     take_halo(early)
     for way in range(2):
         sends.start(block(zs[4]).at[way], in_four.at[way], four_sem.at[way], onward[way])
+    third_sum(0)
     third_send(1)
     take_halo(1 - early)
     for way in range(2):
-        zb = zs[2 if way == 0 else 6]
-        sends.start(block(zb).at[1 - way], in_two.at[way, 1 - way], two_sem.at[way, 1 - way], onward[way])
-    for way in range(2):
-        distance, beyond = ((1, 3), (7, 5))[way]
-        sends.start(
-            total.at[2 + zs[beyond] // 2, way, :, side_cols], in_far.at[way, 0], far_sem.at[way, 0], near_peer[way]
-        )
-        sends.start(
-            total.at[2 + zs[distance] // 2, :, :, side_cols], in_side.at[way], side_sem.at[way], near_peer[way]
-        )
-        sends.start(
-            total.at[2 + zs[beyond] // 2, 1 - way, :, side_cols], in_far.at[way, 1], far_sem.at[way, 1], z_peer[beyond]
-        )
-    third_sum(0)
+        for step in range(2):
+            distance = ((1, 3), (7, 5))[way][step]
+            sends.start(
+                total.at[2 + zs[distance] // 2, :, :, side_cols], in_side.at[way, step], side_sem.at[way, step],
+                near_peer[way],
+            )
     lamp(0)
     sends.arrived(where.at[2], where_sem.at[9], wide_up)
     near = pl.ds(pl.multiple_of(384 - 256 * m, 128), 128)
     for way in range(2):
+        sends.arrived(in_side.at[way, 1], side_sem.at[way, 1], near_peer[1 - way])
         zb = zs[2 if way == 0 else 6]
-        sends.arrived(in_far.at[way, 0], far_sem.at[way, 0], near_peer[1 - way])
-        total[2 + zb // 2, way, :, near] += in_far[way, 0]
+        total[2 + zb // 2, :, :, near] += in_side[way, 1]
+        sends.start(block(zb).at[1 - way], in_two.at[way, 1 - way], two_sem.at[way, 1 - way], onward[way])
+    for way in range(2):
         sends.arrived(in_four.at[way], four_sem.at[way], behind[way])
-        in_four[way] += block(zb)[way]
+        in_four[way] += block(zs[2 if way == 0 else 6])[way]
         sends.start(in_four.at[way], in_two.at[way, way], two_sem.at[way, way], onward[way])
-    scattered = sends.mark()
+    scattered = len(sends.copies)
+    back_second(0)
     third_sum(1)
-    back_second(0)
     lamp(2)
+    back_first(0)
     back_second(1)
-    back_first(0)
     sends.drain(scattered)
 
     for way in range(2):
-        sends.arrived(in_side.at[way], side_sem.at[way], near_peer[1 - way])
-        sends.arrived(in_far.at[way, 1], far_sem.at[way, 1], z_peer[5 if way == 0 else 3])
-        total[2 + zh, 1 - way, :, near] += in_far[way, 1]
-    total[2 + zh, :, :, near] += in_side[0] + in_side[1]
+        sends.arrived(in_side.at[way, 0], side_sem.at[way, 0], near_peer[1 - way])
+    total[2 + zh, :, :, near] += in_side[0, 0] + in_side[1, 0]
     for way in range(2):
         for plane in range(2):
             sends.arrived(in_two.at[way, plane], two_sem.at[way, plane], behind[way])
@@ -584,9 +574,9 @@
         tile[stage + 1] = found
 
     tile_send(0, [None, sibling], 0)
-    back_first(1)
     tile_sum(0, [None, sibling], 0)
     tile_send(1, plane_peer, 1)
+    back_first(1)
     hand_over(0)
     for k in range(MODES):
         part_copy(k).wait_send()
@@ -594,7 +584,7 @@
             first_copy(k, i).wait_send()
     tile_sum(1, plane_peer, 1)
     tile_send(2, z_peer, 16)
-    closing = sends.mark()
+    closing = len(sends.copies)
     hand_over(1)
     sends.drain(closing)
     tile_sum(2, z_peer, 16)
@@ -641,8 +631,7 @@
             v(2, 2, 2, STRIP, 640),
             v(2, STRIP, 512),
             v(2, 2, STRIP, 512),
-            v(2, 2, STRIP, 128),
-            v(2, 2, STRIP, 128),
+            v(2, 2, 2, STRIP, 128),
             v(STRIP, 512),
             v(2, STRIP, 512),
             pltpu.VMEM((16, 2, STRIP, FRAME), bf16),
@@ -670,7 +659,6 @@
             DMA((2, 2)),
             DMA((2,)),
             DMA((2, 2)),
-            DMA((2,)),
             DMA((2, 2)),
             DMA((MODES,)),
             DMA((MODES,)),

time: 91.6 us -> 87.9 us (0.960)
  Pallas kernels: 87 us -> 83.9 us
    pallas_call x1, Pallas kernels: 87 us -> 83.9 us  [update(): pl.pallas_call(update_kernel, out_shape=[pltpu.VMEM((2, STRIP, 512), f32)...]
where the time goes in v6:
time: 87.9 us; the launch traced here: 87.8 us
  Pallas kernels  83.9 us (95%)
  local copies, waits for them, and re-layouts  1.98 us (2%)
  between operations  1.93 us (2%)
    pallas_call x1, Pallas kernels, update(): pl.pallas_call(update_kernel, out_shape=[pltpu.VMEM((2, STRIP, 512), f32)...  83.9 us
    unnamed x2, local copies, waits for them, and re-layouts  1.98 us

profile of v6, /device:TPU:1, one launch (start us, length us, event | category | flops | bytes accessed | tf_op | source)
XLA Modules:
  0.0 87.8 jit_solution(9054392382646567269)
XLA Ops:
  1.9 83.9 %shard_map.77 = (f32[2,32,512]{2,1,0:T(8,128)S(1)}, f32[2,4,256,256]{3,2,1,0:T(8,128)S(1)}) custom-call(f32[2,32,512]{2,1,0:T(8,128)} %obj.1, f32[2,4,256,256]{3,2,1,0:T(8,128)} %probe_in.1, f32[256,256]{1,0:T(8,128)} %bitcast.1, bf16[6,256,256]{2,1,0:T(8,128)(2,1)} %constant.2.clone.tables_in, s32[1,1,1]{2,1,0:T(1,128)S(6)} %copy.12.row_in, ...), custom_call_target="tpu_custom_call" | custom-call | tf_op jit(solution)/shard_map/pallas_call | solution.py:609
  85.8 0.7 copy.10
  86.4 1.3 %copy.11 = f32[2,4,256,256]{3,2,1,0:T(8,128)} copy(f32[2,4,256,256]{3,2,1,0:T(8,128)S(1)} %get-tuple-element.3) | data formatting | bytes 4194304

commit v7 on v6

--- a/solution.py
+++ b/solution.py
@@ -522,8 +522,6 @@
                 total.at[2 + zs[distance] // 2, :, :, side_cols], in_side.at[way, step], side_sem.at[way, step],
                 near_peer[way],
             )
-    lamp(0)
-    sends.arrived(where.at[2], where_sem.at[9], wide_up)
     near = pl.ds(pl.multiple_of(384 - 256 * m, 128), 128)
     for way in range(2):
         sends.arrived(in_side.at[way, 1], side_sem.at[way, 1], near_peer[1 - way])
@@ -537,6 +535,8 @@
     scattered = len(sends.copies)
     back_second(0)
     third_sum(1)
+    lamp(0)
+    sends.arrived(where.at[2], where_sem.at[9], wide_up)
     lamp(2)
     back_first(0)
     back_second(1)
@@ -577,13 +577,13 @@
     tile_sum(0, [None, sibling], 0)
     tile_send(1, plane_peer, 1)
     back_first(1)
-    hand_over(0)
     for k in range(MODES):
         part_copy(k).wait_send()
         for i in range(1, 4):
             first_copy(k, i).wait_send()
     tile_sum(1, plane_peer, 1)
     tile_send(2, z_peer, 16)
+    hand_over(0)
     closing = len(sends.copies)
     hand_over(1)
     sends.drain(closing)

time: 87.9 us -> 87.9 us (level)
  no operation moved by 1% of the time
where the time goes in v7:
time: 87.9 us; the launch traced here: 87.8 us
  Pallas kernels  83.9 us (95%)
  local copies, waits for them, and re-layouts  1.98 us (2%)
  between operations  1.93 us (2%)
    pallas_call x1, Pallas kernels, update(): pl.pallas_call(update_kernel, out_shape=[pltpu.VMEM((2, STRIP, 512), f32)...  83.9 us
    unnamed x2, local copies, waits for them, and re-layouts  1.98 us

profile of v7, /device:TPU:1, one launch (start us, length us, event | category | flops | bytes accessed | tf_op | source)
XLA Modules:
  0.0 87.8 jit_solution(749962488620655241)
XLA Ops:
  1.9 83.9 %shard_map.77 = (f32[2,32,512]{2,1,0:T(8,128)S(1)}, f32[2,4,256,256]{3,2,1,0:T(8,128)S(1)}) custom-call(f32[2,32,512]{2,1,0:T(8,128)} %obj.1, f32[2,4,256,256]{3,2,1,0:T(8,128)} %probe_in.1, f32[256,256]{1,0:T(8,128)} %bitcast.1, bf16[6,256,256]{2,1,0:T(8,128)(2,1)} %constant.2.clone.tables_in, s32[1,1,1]{2,1,0:T(1,128)S(6)} %copy.12.row_in, ...), custom_call_target="tpu_custom_call" | custom-call | tf_op jit(solution)/shard_map/pallas_call | solution.py:609
  85.8 0.7 copy.10
  86.5 1.3 %copy.11 = f32[2,4,256,256]{3,2,1,0:T(8,128)} copy(f32[2,4,256,256]{3,2,1,0:T(8,128)S(1)} %get-tuple-element.3) | data formatting | bytes 4194304
